TPU v7x, 256 devices: a whole 4x4x8 slice. The times are simulated.
256 devices in a mesh: gx: 4 (over x), gy: 4 (over y), gz: 16 (over z, core).
Axes of the slice: x: 4, y: 4, z: 8, core: 2. Of those that a mesh axis runs over, the one named last changes fastest.
Arguments:
- positions: float32 [16384, 3, 128], P(('gx', 'gy', 'gz')), may hold values from 0 to 1
- charges: float32 [16384, 128], P(('gx', 'gy', 'gz')), may hold values from -0.18 to 0.18
- counts: int32 [16384], P(('gx', 'gy', 'gz')), may hold values from 1 to 128
- up_inverse: float32 [64, 64], replicated, may hold values from -0.09375 to 0.09375
- down_inverse: float32 [64, 64], replicated, may hold values from -0.09375 to 0.09375
- inner_surface: float32 [3, 64], replicated, may hold values from 0.15 to 0.85
- outer_surface: float32 [3, 64], replicated, may hold values from -1 to 2, as said below
Outputs:
- potential: float32 [16384, 128], P(('gx', 'gy', 'gz'))
Inputs may be any that keep to these rules, and one draw needn't show every extreme that they name: `outer_surface`: each point lies on the boundary of the cube [-1, 2]^3.
All inputs are finite; a program needn't handle non-finite values.
Results may differ from a plain program's by a relative error of at most 0.0003.
Values sent between devices are 32-bit elements; how exact they have to be, the bound alone decides.
No kernel may reach another device: no remote copies, remote signals or barrier semaphores. Data moves between devices by JAX's collectives and lax.ppermute only.
A program may use at most 64 MiB of HBM per device.

v0:
```python
from functools import partial
import math

import jax
import jax.numpy as jnp
from jax import lax
from jax.sharding import PartitionSpec as P

CX = 4
CY = 4
CZ = 4
PTS = 128
TERMS = 64


SOFTEN = 0.0025
EXACT_DOTS = lax.Precision.HIGHEST


def from_partner(value, axis, stride):
    mask = 2**stride
    pairs = [(source, source ^ mask) for source in range(lax.axis_size(axis))]
    return lax.ppermute(value, axis, pairs)


def kernel(square):
    return 1.0 / jnp.sqrt(square + SOFTEN)


def leaf_blocks(function, arrays, block_size):
    leaf_count = arrays[0].shape[0]
    shaped = tuple(
        (
            member.reshape((leaf_count // block_size, block_size) + member.shape[1:])
            for member in arrays
        )
    )
    result = lax.map(lambda members: function(*members), shaped)
    return result.reshape((leaf_count,) + result.shape[2:])


def upward(outer, position, charge):
    square = jnp.zeros((position.shape[0], outer.shape[1], position.shape[2]), jnp.float32)
    for dimension in range(3):
        spread = outer[dimension][None, :, None] - position[:, dimension, None, :]
        square = square + spread * spread
    return jnp.einsum("nij,nj->ni", kernel(square), charge, precision=EXACT_DOTS)


def downward(outer, position, weight):
    square = jnp.zeros((position.shape[0], position.shape[2], outer.shape[1]), jnp.float32)
    for dimension in range(3):
        spread = position[:, dimension, :, None] - outer[dimension][None, None, :]
        square = square + spread * spread
    return jnp.einsum("nti,ni->nt", kernel(square), weight, precision=EXACT_DOTS)


def pair_potential(target, source, shift, exclude):
    square = jnp.zeros((target.shape[0], target.shape[2], source.shape[2]), jnp.float32)
    for dimension in range(3):
        spread = target[:, dimension, :, None] - source[:, dimension, None, :] - shift[dimension]
        square = square + spread * spread
    weight = kernel(square)
    if exclude:
        weight = weight * (1.0 - jnp.eye(target.shape[2], dtype=jnp.float32))
    return jnp.einsum("nts,ns->nt", weight, source[:, 3, :], precision=EXACT_DOTS)


def allowed(parity, shift):
    return jnp.abs(jnp.floor_divide(parity + shift, 2)) <= 1


def translate(extended, inner, span_x, span_y, span_z):
    parity_x = jnp.arange(span_x, dtype=jnp.int32) % 2
    parity_y = jnp.arange(span_y, dtype=jnp.int32) % 2
    parity_z = jnp.arange(span_z, dtype=jnp.int32) % 2
    terms_count = inner.shape[1]

    def over_x(accum, shift_x):
        slab = lax.dynamic_slice_in_dim(extended, shift_x + 3, span_x, axis=0)
        okay_x = allowed(parity_x, shift_x)
        spread_x = inner[0][:, None] - inner[0][None, :] - shift_x.astype(jnp.float32)
        pieces = []
        masks = []
        matrices = []
        for shift_y in range(-3, 4):
            rows = slab[:, 3 + shift_y : 3 + shift_y + span_y]
            okay_y = allowed(parity_y, shift_y)
            spread_y = inner[1][:, None] - inner[1][None, :] - float(shift_y)
            for shift_z in range(-3, 4):
                pieces.append(rows[:, :, 3 + shift_z : 3 + shift_z + span_z])
                okay_z = allowed(parity_z, shift_z)
                spread_z = inner[2][:, None] - inner[2][None, :] - float(shift_z)
                matrices.append(
                    kernel(spread_x * spread_x + spread_y * spread_y + spread_z * spread_z)
                )
                extent = jnp.maximum(jnp.maximum(jnp.abs(shift_x), abs(shift_y)), abs(shift_z))
                masks.append(
                    okay_x[:, None, None]
                    & okay_y[None, :, None]
                    & okay_z[None, None, :]
                    & (extent >= 2)
                )
        stacked = jnp.stack(pieces)
        mask = jnp.stack(masks)
        weighted = stacked * mask[..., None].astype(jnp.float32)
        accum = accum + jnp.einsum(
            "oxyzj,oij->xyzi", weighted, jnp.stack(matrices), precision=EXACT_DOTS
        )
        return (accum, None)

    start = jnp.zeros((span_x, span_y, span_z, terms_count), jnp.float32)
    result, _ = lax.scan(over_x, start, jnp.arange(-3, 4, dtype=jnp.int32))
    return result


def axis_bits():
    low_bits = lax.axis_size("gz").bit_length() - 1
    mid_bits = lax.axis_size("gy").bit_length() - 1
    high_bits = lax.axis_size("gx").bit_length() - 1
    return (low_bits, mid_bits, high_bits)


def flip(rising_dens, rising_points, falling_dens, falling_points, global_bit):
    low_bits, mid_bits, high_bits = axis_bits()
    if global_bit < low_bits:
        return from_partner(
            (rising_dens, rising_points, falling_dens, falling_points), "gz", global_bit
        )
    if global_bit < low_bits + mid_bits:
        return from_partner(
            (rising_dens, rising_points, falling_dens, falling_points), "gy", global_bit - low_bits
        )
    return from_partner(
        (rising_dens, rising_points, falling_dens, falling_points),
        "gx",
        global_bit - low_bits - mid_bits,
    )


def box_place(device, dimension, total_bits):
    place = jnp.zeros((), jnp.int32)
    for bit_rank, global_bit in enumerate(range(dimension, total_bits, 3)):
        place = place + jnp.left_shift(
            jnp.bitwise_and(jnp.right_shift(device, global_bit), 1), bit_rank
        )
    return place


def extend(density, points, dimension, layers, device, total_bits):
    position = box_place(device, dimension, total_bits)
    dens_size = density.shape[dimension]
    point_size = points.shape[dimension]
    rising_dens = lax.slice_in_dim(density, dens_size - layers, dens_size, axis=dimension)
    rising_points = lax.slice_in_dim(points, point_size - 1, point_size, axis=dimension)
    falling_dens = lax.slice_in_dim(density, 0, layers, axis=dimension)
    falling_points = lax.slice_in_dim(points, 0, 1, axis=dimension)
    lower_dens = jnp.zeros_like(rising_dens)
    lower_points = jnp.zeros_like(rising_points)
    upper_dens = jnp.zeros_like(falling_dens)
    upper_points = jnp.zeros_like(falling_points)
    carried = (rising_dens, rising_points, falling_dens, falling_points)
    for bit_rank, global_bit in enumerate(range(dimension, total_bits, 3)):
        carried = flip(carried[0], carried[1], carried[2], carried[3], global_bit)
        got_lower = (carried[0], carried[1])
        got_upper = (carried[2], carried[3])
        bit_value = jnp.bitwise_and(jnp.right_shift(position, bit_rank), 1)
        below_bits = jnp.bitwise_and(position, (1 << bit_rank) - 1)
        from_lower = (bit_value == 1) & (below_bits == 0)
        from_upper = (bit_value == 0) & (below_bits == (1 << bit_rank) - 1)
        lower_dens = jnp.where(from_lower, got_lower[0], lower_dens)
        lower_points = jnp.where(from_lower, got_lower[1], lower_points)
        upper_dens = jnp.where(from_upper, got_upper[0], upper_dens)
        upper_points = jnp.where(from_upper, got_upper[1], upper_points)
    density = jnp.concatenate([lower_dens, density, upper_dens], axis=dimension)
    points = jnp.concatenate([lower_points, points, upper_points], axis=dimension)
    return (density, points)


def per_device(positions, charges, counts, up_inverse, down_inverse, inner_surface, outer_surface):
    leaf_total = positions.shape[0]
    block_rows = math.gcd(leaf_total, 64)
    live = (jnp.arange(PTS, dtype=jnp.int32)[None, :] < counts[:, None]).astype(jnp.float32)
    source = charges * live
    check_up = leaf_blocks(partial(upward, outer_surface), (positions, source), block_rows)
    density = jnp.dot(
        check_up, up_inverse.T, preferred_element_type=jnp.float32, precision=EXACT_DOTS
    )
    dens_grid = density.reshape(CX, CY, CZ, TERMS)
    point_grid = jnp.concatenate([positions, source[:, None, :]], axis=1).reshape(
        CX, CY, CZ, 4, PTS
    )
    low_bits, mid_bits, high_bits = axis_bits()
    total_bits = low_bits + mid_bits + high_bits
    device = (lax.axis_index("gx") * lax.axis_size("gy") + lax.axis_index("gy")) * lax.axis_size(
        "gz"
    ) + lax.axis_index("gz")
    layers = 2
    for dimension in range(3):
        dens_grid, point_grid = extend(dens_grid, point_grid, dimension, layers, device, total_bits)
    dens_grid = jnp.pad(dens_grid, ((1, 1), (1, 1), (1, 1), (0, 0)))
    near = jnp.zeros((leaf_total, PTS), jnp.float32)
    for shift_x in range(-1, 2):
        for shift_y in range(-1, 2):
            for shift_z in range(-1, 2):
                window = point_grid[
                    1 + shift_x : 1 + shift_x + CX,
                    1 + shift_y : 1 + shift_y + CY,
                    1 + shift_z : 1 + shift_z + CZ,
                ]
                window = window.reshape(leaf_total, 4, PTS)
                exclude = shift_x == 0 and shift_y == 0 and (shift_z == 0)
                near = near + leaf_blocks(
                    partial(pair_potential, shift=(shift_x, shift_y, shift_z), exclude=exclude),
                    (positions, window),
                    block_rows,
                )
    check_down = translate(dens_grid, inner_surface, CX, CY, CZ).reshape(leaf_total, TERMS)
    local = jnp.dot(
        check_down, down_inverse.T, preferred_element_type=jnp.float32, precision=EXACT_DOTS
    )
    far = leaf_blocks(partial(downward, outer_surface), (positions, local), block_rows)
    return live * (near + far)


def solution(mesh):
    in_specs = (
        P(("gx", "gy", "gz"), None, None),
        P(("gx", "gy", "gz"), None),
        P(("gx", "gy", "gz")),
        P(),
        P(),
        P(),
        P(),
    )
    out_specs = P(("gx", "gy", "gz"), None)
    return jax.shard_map(
        per_device, mesh=mesh, in_specs=in_specs, out_specs=out_specs, check_vma=False
    )
```

profile of v0, /device:TPU:16, one launch (start us, length us, event | category | flops | bytes accessed | tf_op | source)
XLA Modules:
  0.0 583.0 jit_solution(4224260357954733622)
XLA Ops:
  63.4 10.2 %fusion.235 = f32[64,1,128]{2,1,0:T(1,128)S(1)} fusion(f32[64,128,1]{1,2,0:T(1,128)S(1)} %bitcast.858, f32[64,128]{1,0:T(8,128)S(1)} %get-tuple-element.1083, f32[64,128]{1,0:T(8,128)S(1)} %get-tuple-element.1084, f32[64,128]{1,0:T(8,128)S(1)} %get-tuple-element.1081, f32[64,128]{1,0:T(8,128)S(1)} %get-tuple-element.1106, ...), kind=kOutput, calls=%fused_computation.501 | convolution fusion | flops 23068672 | bytes 262144 | tf_op jit(solution)/shard_map/while/body/eval_jaxpr/nts,ns->nt/dot_general | solution.py:66
  90.9 215.0 %while.12 = (s32[]{:T(128)}, f32[4,4,4,64]{3,2,0,1:T(4,128)S(1)}, s32[7]{0:T(128)}, f32[10,10,10,64]{3,2,0,1:T(8,128)S(1)}, f32[3,64]{1,0:T(4,128)S(1)}, /*index...) while((s32[]{:T(128)}, f32[4,4,4,64]{3,2,0,1:T(4,128)S(1)}, ...), condition=%wide.region_1.2_spmd.clone.clone, body=%wide.region_0.1_spmd.clone.clone.sunk | while | flops 156711040 | bytes 9905873 | solution.py:113
  325.5 10.2 %fusion.195 = f32[64,1,128]{2,1,0:T(1,128)S(1)} fusion(f32[64,128,1]{1,2,0:T(1,128)S(1)} %bitcast.851, f32[64,128]{1,0:T(8,128)S(1)} %get-tuple-element.1095, f32[64,128]{1,0:T(8,128)S(1)} %get-tuple-element.1096, f32[64,128]{1,0:T(8,128)S(1)} %get-tuple-element.1093, f32[64,128]{1,0:T(8,128)S(1)} %get-tuple-element.1106, ...), kind=kOutput, calls=%fused_computation.461 | convolution fusion | flops 24117248 | bytes 262144 | tf_op jit(solution)/shard_map/while/body/eval_jaxpr/nts,ns->nt/dot_general | solution.py:66
  335.7 10.2 %fusion.274 = f32[64,1,128]{2,1,0:T(1,128)S(1)} fusion(f32[64,128,1]{1,2,0:T(1,128)S(1)} %bitcast.852, f32[64,128]{1,0:T(8,128)S(1)} %get-tuple-element.1071, f32[64,128]{1,0:T(8,128)S(1)} %get-tuple-element.1072, f32[64,128]{1,0:T(8,128)S(1)} %get-tuple-element.1069, f32[64,128]{1,0:T(8,128)S(1)} %get-tuple-element.1106, ...), kind=kOutput, calls=%fused_computation.540 | convolution fusion | flops 24117248 | bytes 262144 | tf_op jit(solution)/shard_map/while/body/eval_jaxpr/nts,ns->nt/dot_general | solution.py:66
  345.9 10.2 %fusion.314 = f32[64,1,128]{2,1,0:T(1,128)S(1)} fusion(f32[64,128,1]{1,2,0:T(1,128)S(1)} %bitcast.853, f32[64,128]{1,0:T(8,128)S(1)} %get-tuple-element.1059, f32[64,128]{1,0:T(8,128)S(1)} %get-tuple-element.1060, f32[64,128]{1,0:T(8,128)S(1)} %get-tuple-element.1057, f32[64,128]{1,0:T(8,128)S(1)} %get-tuple-element.1106, ...), kind=kOutput, calls=%fused_computation.580 | convolution fusion | flops 23068672 | bytes 262144 | tf_op jit(solution)/shard_map/while/body/eval_jaxpr/nts,ns->nt/dot_general | solution.py:66
  356.2 10.2 %fusion.427 = f32[64,1,128]{2,1,0:T(1,128)S(1)} fusion(f32[64,128,1]{1,2,0:T(1,128)S(1)} %bitcast.854, f32[64,128]{1,0:T(8,128)S(1)} %get-tuple-element.1027, f32[64,128]{1,0:T(8,128)S(1)} %get-tuple-element.1028, f32[64,128]{1,0:T(8,128)S(1)} %get-tuple-element.1025, f32[64,128]{1,0:T(8,128)S(1)} %get-tuple-element.1106, ...), kind=kOutput, calls=%fused_computation.693 | convolution fusion | flops 24117248 | bytes 262144 | tf_op jit(solution)/shard_map/while/body/eval_jaxpr/nts,ns->nt/dot_general | solution.py:66
  366.4 10.2 %fusion.506 = f32[64,1,128]{2,1,0:T(1,128)S(1)} fusion(f32[64,128,1]{1,2,0:T(1,128)S(1)} %bitcast.855, f32[64,128]{1,0:T(8,128)S(1)} %get-tuple-element.997, f32[64,128]{1,0:T(8,128)S(1)} %get-tuple-element.998, f32[64,128]{1,0:T(8,128)S(1)} %get-tuple-element.995, f32[64,128]{1,0:T(8,128)S(1)} %get-tuple-element.1106, ...), kind=kOutput, calls=%fused_computation.772 | convolution fusion | flops 24117248 | bytes 262144 | tf_op jit(solution)/shard_map/while/body/eval_jaxpr/nts,ns->nt/dot_general | solution.py:66
  397.2 10.2 %fusion.181 = f32[64,1,128]{2,1,0:T(1,128)S(1)} fusion(f32[64,128,1]{1,2,0:T(1,128)S(1)} %bitcast.834, f32[64,128]{1,0:T(8,128)S(1)} %get-tuple-element.1099, f32[64,128]{1,0:T(8,128)S(1)} %get-tuple-element.1100, f32[64,128]{1,0:T(8,128)S(1)} %get-tuple-element.1097, f32[64,128]{1,0:T(8,128)S(1)} %get-tuple-element.1106, ...), kind=kOutput, calls=%fused_computation.447 | convolution fusion | flops 25165824 | bytes 262144 | tf_op jit(solution)/shard_map/while/body/eval_jaxpr/nts,ns->nt/dot_general | solution.py:66
  407.4 10.2 %fusion.208 = f32[64,1,128]{2,1,0:T(1,128)S(1)} fusion(f32[64,128,1]{1,2,0:T(1,128)S(1)} %bitcast.835, f32[64,128]{1,0:T(8,128)S(1)} %get-tuple-element.1091, f32[64,128]{1,0:T(8,128)S(1)} %get-tuple-element.1092, f32[64,128]{1,0:T(8,128)S(1)} %get-tuple-element.1089, f32[64,128]{1,0:T(8,128)S(1)} %get-tuple-element.1106, ...), kind=kOutput, calls=%fused_computation.474 | convolution fusion | flops 25165824 | bytes 262144 | tf_op jit(solution)/shard_map/while/body/eval_jaxpr/nts,ns->nt/dot_general | solution.py:66
  417.7 10.2 %fusion.222 = f32[64,1,128]{2,1,0:T(1,128)S(1)} fusion(f32[64,128,1]{1,2,0:T(1,128)S(1)} %bitcast.836, f32[64,128]{1,0:T(8,128)S(1)} %get-tuple-element.1087, f32[64,128]{1,0:T(8,128)S(1)} %get-tuple-element.1088, f32[64,128]{1,0:T(8,128)S(1)} %get-tuple-element.1085, f32[64,128]{1,0:T(8,128)S(1)} %get-tuple-element.1106, ...), kind=kOutput, calls=%fused_computation.488 | convolution fusion | flops 24117248 | bytes 262144 | tf_op jit(solution)/shard_map/while/body/eval_jaxpr/nts,ns->nt/dot_general | solution.py:66
  427.9 10.2 %fusion.247 = f32[64,1,128]{2,1,0:T(1,128)S(1)} fusion(f32[64,128,1]{1,2,0:T(1,128)S(1)} %bitcast.837, f32[64,128]{1,0:T(8,128)S(1)} %get-tuple-element.1079, f32[64,128]{1,0:T(8,128)S(1)} %get-tuple-element.1080, f32[64,128]{1,0:T(8,128)S(1)} %get-tuple-element.1077, f32[64,128]{1,0:T(8,128)S(1)} %get-tuple-element.1106, ...), kind=kOutput, calls=%fused_computation.513 | convolution fusion | flops 24117248 | bytes 262144 | tf_op jit(solution)/shard_map/while/body/eval_jaxpr/nts,ns->nt/dot_general | solution.py:66
  438.1 10.3 %fusion.260 = f32[64,1,128]{2,1,0:T(1,128)S(1)} fusion(f32[64,128,1]{1,2,0:T(1,128)S(1)} %bitcast.838, f32[64,128]{1,0:T(8,128)S(1)} %get-tuple-element.1075, f32[64,128]{1,0:T(8,128)S(1)} %get-tuple-element.1076, f32[64,128]{1,0:T(8,128)S(1)} %get-tuple-element.1073, f32[64,128]{1,0:T(8,128)S(1)} %get-tuple-element.1106, ...), kind=kOutput, calls=%fused_computation.526 | convolution fusion | flops 25165824 | bytes 262144 | tf_op jit(solution)/shard_map/while/body/eval_jaxpr/nts,ns->nt/dot_general | solution.py:66
  448.4 10.2 %fusion.287 = f32[64,1,128]{2,1,0:T(1,128)S(1)} fusion(f32[64,128,1]{1,2,0:T(1,128)S(1)} %bitcast.839, f32[64,128]{1,0:T(8,128)S(1)} %get-tuple-element.1067, f32[64,128]{1,0:T(8,128)S(1)} %get-tuple-element.1068, f32[64,128]{1,0:T(8,128)S(1)} %get-tuple-element.1065, f32[64,128]{1,0:T(8,128)S(1)} %get-tuple-element.1106, ...), kind=kOutput, calls=%fused_computation.553 | convolution fusion | flops 25165824 | bytes 262144 | tf_op jit(solution)/shard_map/while/body/eval_jaxpr/nts,ns->nt/dot_general | solution.py:66
  468.9 10.2 %fusion.326 = f32[64,1,128]{2,1,0:T(1,128)S(1)} fusion(f32[64,128,1]{1,2,0:T(1,128)S(1)} %bitcast.841, f32[64,128]{1,0:T(8,128)S(1)} %get-tuple-element.1055, f32[64,128]{1,0:T(8,128)S(1)} %get-tuple-element.1056, f32[64,128]{1,0:T(8,128)S(1)} %get-tuple-element.1053, f32[64,128]{1,0:T(8,128)S(1)} %get-tuple-element.1106, ...), kind=kOutput, calls=%fused_computation.592 | convolution fusion | flops 24117248 | bytes 262144 | tf_op jit(solution)/shard_map/while/body/eval_jaxpr/nts,ns->nt/dot_general | solution.py:66
  479.1 10.2 %fusion.339 = f32[64,1,128]{2,1,0:T(1,128)S(1)} fusion(f32[64,128,1]{1,2,0:T(1,128)S(1)} %bitcast.842, f32[64,128]{1,0:T(8,128)S(1)} %get-tuple-element.1051, f32[64,128]{1,0:T(8,128)S(1)} %get-tuple-element.1052, f32[64,128]{1,0:T(8,128)S(1)} %get-tuple-element.1049, f32[64,128]{1,0:T(8,128)S(1)} %get-tuple-element.1106, ...), kind=kOutput, calls=%fused_computation.605 | convolution fusion | flops 23068672 | bytes 262144 | tf_op jit(solution)/shard_map/while/body/eval_jaxpr/nts,ns->nt/dot_general | solution.py:66
  489.4 10.2 %fusion.363 = f32[64,1,128]{2,1,0:T(1,128)S(1)} fusion(f32[64,128,1]{1,2,0:T(1,128)S(1)} %bitcast.843, f32[64,128]{1,0:T(8,128)S(1)} %get-tuple-element.1047, f32[64,128]{1,0:T(8,128)S(1)} %get-tuple-element.1048, f32[64,128]{1,0:T(8,128)S(1)} %get-tuple-element.1045, f32[64,128]{1,0:T(8,128)S(1)} %get-tuple-element.1106, ...), kind=kOutput, calls=%fused_computation.629 | convolution fusion | flops 23068672 | bytes 262144 | tf_op jit(solution)/shard_map/while/body/eval_jaxpr/nts,ns->nt/dot_general | solution.py:66
  499.6 10.2 %fusion.375 = f32[64,1,128]{2,1,0:T(1,128)S(1)} fusion(f32[64,128,1]{1,2,0:T(1,128)S(1)} %bitcast.844, f32[64,128]{1,0:T(8,128)S(1)} %get-tuple-element.1043, f32[64,128]{1,0:T(8,128)S(1)} %get-tuple-element.1044, f32[64,128]{1,0:T(8,128)S(1)} %get-tuple-element.1041, f32[64,128]{1,0:T(8,128)S(1)} %get-tuple-element.1106, ...), kind=kOutput, calls=%fused_computation.641 | convolution fusion | flops 24117248 | bytes 262144 | tf_op jit(solution)/shard_map/while/body/eval_jaxpr/nts,ns->nt/dot_general | solution.py:66
  509.8 10.2 %fusion.400 = f32[64,1,128]{2,1,0:T(1,128)S(1)} fusion(f32[64,128,1]{1,2,0:T(1,128)S(1)} %bitcast.845, f32[64,128]{1,0:T(8,128)S(1)} %get-tuple-element.1035, f32[64,128]{1,0:T(8,128)S(1)} %get-tuple-element.1036, f32[64,128]{1,0:T(8,128)S(1)} %get-tuple-element.1033, f32[64,128]{1,0:T(8,128)S(1)} %get-tuple-element.1106, ...), kind=kOutput, calls=%fused_computation.666 | convolution fusion | flops 24117248 | bytes 262144 | tf_op jit(solution)/shard_map/while/body/eval_jaxpr/nts,ns->nt/dot_general | solution.py:66
  520.1 10.3 %fusion.413 = f32[64,1,128]{2,1,0:T(1,128)S(1)} fusion(f32[64,128,1]{1,2,0:T(1,128)S(1)} %bitcast.846, f32[64,128]{1,0:T(8,128)S(1)} %get-tuple-element.1031, f32[64,128]{1,0:T(8,128)S(1)} %get-tuple-element.1032, f32[64,128]{1,0:T(8,128)S(1)} %get-tuple-element.1029, f32[64,128]{1,0:T(8,128)S(1)} %get-tuple-element.1106, ...), kind=kOutput, calls=%fused_computation.679 | convolution fusion | flops 25165824 | bytes 262144 | tf_op jit(solution)/shard_map/while/body/eval_jaxpr/nts,ns->nt/dot_general | solution.py:66
  530.3 10.2 %fusion.440 = f32[64,1,128]{2,1,0:T(1,128)S(1)} fusion(f32[64,128,1]{1,2,0:T(1,128)S(1)} %bitcast.847, f32[64,128]{1,0:T(8,128)S(1)} %get-tuple-element.1023, f32[64,128]{1,0:T(8,128)S(1)} %get-tuple-element.1024, f32[64,128]{1,0:T(8,128)S(1)} %get-tuple-element.1021, f32[64,128]{1,0:T(8,128)S(1)} %get-tuple-element.1106, ...), kind=kOutput, calls=%fused_computation.706 | convolution fusion | flops 25165824 | bytes 262144 | tf_op jit(solution)/shard_map/while/body/eval_jaxpr/nts,ns->nt/dot_general | solution.py:66
  540.6 10.5 %fusion.454 = f32[64,1,128]{2,1,0:T(1,128)S(1)} fusion(f32[64,128,1]{1,2,0:T(1,128)S(1)} %bitcast.848, f32[64,128]{1,0:T(8,128)S(1)} %get-tuple-element.1019, f32[64,128]{1,0:T(8,128)S(1)} %get-tuple-element.1020, f32[64,128]{1,0:T(8,128)S(1)} %get-tuple-element.1017, f32[64,128]{1,0:T(8,128)S(1)} %get-tuple-element.1106, ...), kind=kOutput, calls=%fused_computation.720 | convolution fusion | flops 24117248 | bytes 262144 | tf_op jit(solution)/shard_map/while/body/eval_jaxpr/nts,ns->nt/dot_general | solution.py:66
  551.1 10.2 %fusion.479 = f32[64,1,128]{2,1,0:T(1,128)S(1)} fusion(f32[64,128,1]{1,2,0:T(1,128)S(1)} %bitcast.849, f32[64,128]{1,0:T(8,128)S(1)} %get-tuple-element.1009, f32[64,128]{1,0:T(8,128)S(1)} %get-tuple-element.1010, f32[64,128]{1,0:T(8,128)S(1)} %get-tuple-element.1007, f32[64,128]{1,0:T(8,128)S(1)} %get-tuple-element.1106, ...), kind=kOutput, calls=%fused_computation.745 | convolution fusion | flops 24117248 | bytes 262144 | tf_op jit(solution)/shard_map/while/body/eval_jaxpr/nts,ns->nt/dot_general | solution.py:66
  561.3 10.3 %fusion.492 = f32[64,1,128]{2,1,0:T(1,128)S(1)} fusion(f32[64,128,1]{1,2,0:T(1,128)S(1)} %bitcast.850, f32[64,128]{1,0:T(8,128)S(1)} %get-tuple-element.1005, f32[64,128]{1,0:T(8,128)S(1)} %get-tuple-element.1006, f32[64,128]{1,0:T(8,128)S(1)} %get-tuple-element.1003, f32[64,128]{1,0:T(8,128)S(1)} %get-tuple-element.1106, ...), kind=kOutput, calls=%fused_computation.758 | convolution fusion | flops 25165824 | bytes 262144 | tf_op jit(solution)/shard_map/while/body/eval_jaxpr/nts,ns->nt/dot_general | solution.py:66
  571.6 10.2 %fusion.519 = f32[64,1,128]{2,1,0:T(1,128)S(1)} fusion(f32[64,128,1]{1,2,0:T(1,128)S(1)} %bitcast.833, f32[64,128]{1,0:T(8,128)S(1)} %get-tuple-element.1001, f32[64,128]{1,0:T(8,128)S(1)} %get-tuple-element.1106, f32[64,128]{1,0:T(8,128)S(1)} %get-tuple-element.1002, f32[64,128]{1,0:T(8,128)S(1)} %get-tuple-element.1107, ...), kind=kOutput, calls=%fused_computation.785 | convolution fusion | flops 25165824 | bytes 262144 | tf_op jit(solution)/shard_map/while/body/eval_jaxpr/nts,ns->nt/dot_general | solution.py:66
  (1317 shorter events, 321.2 us)
Async XLA Ops:
  6.8 8.4 %collective-permute-start.16 = (f32[2,4,4,64]{3,2,0,1:T(4,128)S(1)}, f32[2,4,4,64]{3,2,0,1:T(4,128)S(1)}, u32[]{:S(2)}, u32[]{:S(2)}) collective-permute-start(f32[2,4,4,64]{3,2,0,1:T(4,128)S(1)} %copy.76), channel_id=1, source_target_pairs={{0,1},{1,0},{2,3},{3,2},{4,5},{5,4},{6,7},{7,6},{8,9},{9,8},{10,11... | collective-permute-start | bytes 24584 | tf_op jit(solution)/shard_map/ppermute | solution.py:23
  7.9 8.9 %collective-permute-start.20 = (f32[2,4,4,64]{3,2,0,1:T(4,128)S(1)}, f32[2,4,4,64]{3,2,0,1:T(4,128)S(1)}, u32[]{:S(2)}, u32[]{:S(2)}) collective-permute-start(f32[2,4,4,64]{3,2,0,1:T(4,128)S(1)} %collective-permute-done.19), channel_id=1, source_target_pairs={{0,8},{1,9},{2,10},{3,11},{4,12},{5,13},{6,14},{7,15},{8,0},{9,1},... | collective-permute-start | bytes 24584 | tf_op jit(solution)/shard_map/ppermute | solution.py:23
  15.2 7.7 %collective-permute-start.17 = (f32[2,4,4,64]{3,2,0,1:T(4,128)S(1)}, f32[2,4,4,64]{3,2,0,1:T(4,128)S(1)}, u32[]{:S(2)}, u32[]{:S(2)}) collective-permute-start(f32[2,4,4,64]{3,2,0,1:T(4,128)S(1)} %collective-permute-done.16), channel_id=1, source_target_pairs={{0,8},{1,9},{2,10},{3,11},{4,12},{5,13},{6,14},{7,15},{8,0},{9,1},... | collective-permute-start | bytes 24584 | tf_op jit(solution)/shard_map/ppermute | solution.py:23
  16.8 7.6 %collective-permute-start.21 = (f32[2,4,4,64]{3,2,0,1:T(4,128)S(1)}, f32[2,4,4,64]{3,2,0,1:T(4,128)S(1)}, u32[]{:S(2)}, u32[]{:S(2)}) collective-permute-start(f32[2,4,4,64]{3,2,0,1:T(4,128)S(1)} %collective-permute-done.20), channel_id=1, source_target_pairs={{0,64},{64,0},{128,192},{192,128},{1,65},{65,1},{129,193},{193,129... | collective-permute-start | bytes 24584 | tf_op jit(solution)/shard_map/ppermute | solution.py:23
  18.3 23.7 %collective-permute-start.3 = (f32[1,4,4,4,128]{4,2,1,0,3:T(4,128)S(1)}, f32[1,4,4,4,128]{4,2,1,0,3:T(4,128)S(1)}, u32[]{:S(2)}, u32[]{:S(2)}) collective-permute-start(f32[1,4,4,4,128]{4,2,1,0,3:T(4,128)S(1)} %bitcast.832), channel_id=1, source_target_pairs={{0,1},{1,0},{2,3},{3,2},{4,5},{5,4},{6,7},{7,6},{8,9},{9,8},{10,11... | collective-permute-start | bytes 98312 | tf_op jit(solution)/shard_map/ppermute | solution.py:23
  18.4 25.6 %collective-permute-start = (f32[1,4,4,4,128]{4,2,1,0,3:T(4,128)S(1)}, f32[1,4,4,4,128]{4,2,1,0,3:T(4,128)S(1)}, u32[]{:S(2)}, u32[]{:S(2)}) collective-permute-start(f32[1,4,4,4,128]{4,2,1,0,3:T(4,128)S(1)} %bitcast.831), channel_id=1, source_target_pairs={{0,1},{1,0},{2,3},{3,2},{4,5},{5,4},{6,7},{7,6},{8,9},{9,8},{10,11... | collective-permute-start | bytes 98312 | tf_op jit(solution)/shard_map/ppermute | solution.py:23
  27.9 20.3 %collective-permute-start.22 = (f32[8,2,4,64]{3,2,0,1:T(4,128)S(1)}, f32[8,2,4,64]{3,2,0,1:T(4,128)S(1)}, u32[]{:S(2)}, u32[]{:S(2)}) collective-permute-start(f32[8,2,4,64]{3,2,0,1:T(4,128)S(1)} %get-tuple-element.1108), channel_id=1, source_target_pairs={{0,2},{1,3},{2,0},{3,1},{4,6},{5,7},{6,4},{7,5},{8,10},{9,11},{10,... | collective-permute-start | bytes 49160 | tf_op jit(solution)/shard_map/ppermute | solution.py:23
  30.7 18.2 %collective-permute-start.26 = (f32[8,2,4,64]{3,2,0,1:T(4,128)S(1)}, f32[8,2,4,64]{3,2,0,1:T(4,128)S(1)}, u32[]{:S(2)}, u32[]{:S(2)}) collective-permute-start(f32[8,2,4,64]{3,2,0,1:T(4,128)S(1)} %collective-permute-done.25), channel_id=1, source_target_pairs={{0,16},{16,0},{32,48},{48,32},{1,17},{17,1},{33,49},{49,33},{2,18}... | collective-permute-start | bytes 49160 | tf_op jit(solution)/shard_map/ppermute | solution.py:23
  42.1 13.1 %collective-permute-start.4 = (f32[1,4,4,4,128]{4,2,1,0,3:T(4,128)S(1)}, f32[1,4,4,4,128]{4,2,1,0,3:T(4,128)S(1)}, u32[]{:S(2)}, u32[]{:S(2)}) collective-permute-start(f32[1,4,4,4,128]{4,2,1,0,3:T(4,128)S(1)} %collective-permute-done.3), channel_id=1, source_target_pairs={{0,8},{1,9},{2,10},{3,11},{4,12},{5,13},{6,14},{7,15},{8,0},{9,1},... | collective-permute-start | bytes 98312 | tf_op jit(solution)/shard_map/ppermute | solution.py:23
  44.0 11.7 %collective-permute-start.1 = (f32[1,4,4,4,128]{4,2,1,0,3:T(4,128)S(1)}, f32[1,4,4,4,128]{4,2,1,0,3:T(4,128)S(1)}, u32[]{:S(2)}, u32[]{:S(2)}) collective-permute-start(f32[1,4,4,4,128]{4,2,1,0,3:T(4,128)S(1)} %collective-permute-done), channel_id=1, source_target_pairs={{0,8},{1,9},{2,10},{3,11},{4,12},{5,13},{6,14},{7,15},{8,0},{9,1},... | collective-permute-start | bytes 98312 | tf_op jit(solution)/shard_map/ppermute | solution.py:23
  48.9 8.2 %collective-permute-start.27 = (f32[8,2,4,64]{3,2,0,1:T(4,128)S(1)}, f32[8,2,4,64]{3,2,0,1:T(4,128)S(1)}, u32[]{:S(2)}, u32[]{:S(2)}) collective-permute-start(f32[8,2,4,64]{3,2,0,1:T(4,128)S(1)} %collective-permute-done.26), channel_id=1, source_target_pairs={{0,128},{64,192},{128,0},{192,64},{1,129},{65,193},{129,1},{193,65... | collective-permute-start | bytes 49160 | tf_op jit(solution)/shard_map/ppermute | solution.py:23
  55.1 5.9 %collective-permute-start.5 = (f32[1,4,4,4,128]{4,2,1,0,3:T(4,128)S(1)}, f32[1,4,4,4,128]{4,2,1,0,3:T(4,128)S(1)}, u32[]{:S(2)}, u32[]{:S(2)}) collective-permute-start(f32[1,4,4,4,128]{4,2,1,0,3:T(4,128)S(1)} %collective-permute-done.4), channel_id=1, source_target_pairs={{0,64},{64,0},{128,192},{192,128},{1,65},{65,1},{129,193},{193,129... | collective-permute-start | bytes 98312 | tf_op jit(solution)/shard_map/ppermute | solution.py:23
  58.0 15.6 %collective-permute-start.30 = (f32[8,8,2,64]{3,2,0,1:T(2,128)S(1)}, f32[8,8,2,64]{3,2,0,1:T(2,128)S(1)}, u32[]{:S(2)}, u32[]{:S(2)}) collective-permute-start(f32[8,8,2,64]{3,2,0,1:T(2,128)S(1)} %get-tuple-element.1104), channel_id=1, source_target_pairs={{0,4},{1,5},{2,6},{3,7},{4,0},{5,1},{6,2},{7,3},{8,12},{9,13},{10,... | collective-permute-start | bytes 98312 | tf_op jit(solution)/shard_map/ppermute | solution.py:23
  59.6 24.7 %collective-permute-start.28 = (f32[8,8,2,64]{3,2,0,1:T(2,128)S(1)}, f32[8,8,2,64]{3,2,0,1:T(2,128)S(1)}, u32[]{:S(2)}, u32[]{:S(2)}) collective-permute-start(f32[8,8,2,64]{3,2,0,1:T(2,128)S(1)} %get-tuple-element.1103), channel_id=1, source_target_pairs={{0,4},{1,5},{2,6},{3,7},{4,0},{5,1},{6,2},{7,3},{8,12},{9,13},{10,... | collective-permute-start | bytes 98312 | tf_op jit(solution)/shard_map/ppermute | solution.py:23
  61.2 244.7 %collective-permute-start.9 = (f32[6,1,4,4,128]{4,2,1,0,3:T(4,128)S(1)}, f32[6,1,4,4,128]{4,2,1,0,3:T(4,128)S(1)}, u32[]{:S(2)}, u32[]{:S(2)}) collective-permute-start(f32[6,1,4,4,128]{4,2,1,0,3:T(4,128)S(1)} %get-tuple-element.994), channel_id=1, source_target_pairs={{0,2},{1,3},{2,0},{3,1},{4,6},{5,7},{6,4},{7,5},{8,10},{9,11},{10,... | collective-permute-start | bytes 147464 | tf_op jit(solution)/shard_map/ppermute | solution.py:23
  62.3 246.0 %collective-permute-start.6 = (f32[6,1,4,4,128]{4,2,1,0,3:T(4,128)S(1)}, f32[6,1,4,4,128]{4,2,1,0,3:T(4,128)S(1)}, u32[]{:S(2)}, u32[]{:S(2)}) collective-permute-start(f32[6,1,4,4,128]{4,2,1,0,3:T(4,128)S(1)} %get-tuple-element.993), channel_id=1, source_target_pairs={{0,2},{1,3},{2,0},{3,1},{4,6},{5,7},{6,4},{7,5},{8,10},{9,11},{10,... | collective-permute-start | bytes 147464 | tf_op jit(solution)/shard_map/ppermute | solution.py:23
  73.6 14.3 %collective-permute-start.31 = (f32[8,8,2,64]{3,2,0,1:T(2,128)S(1)}, f32[8,8,2,64]{3,2,0,1:T(2,128)S(1)}, u32[]{:S(2)}, u32[]{:S(2)}) collective-permute-start(f32[8,8,2,64]{3,2,0,1:T(2,128)S(1)} %collective-permute-done.30), channel_id=1, source_target_pairs={{0,32},{16,48},{32,0},{48,16},{1,33},{17,49},{33,1},{49,17},{2,34}... | collective-permute-start | bytes 98312 | tf_op jit(solution)/shard_map/ppermute | solution.py:23
  84.3 6.2 %collective-permute-start.29 = (f32[8,8,2,64]{3,2,0,1:T(2,128)S(1)}, f32[8,8,2,64]{3,2,0,1:T(2,128)S(1)}, u32[]{:S(2)}, u32[]{:S(2)}) collective-permute-start(f32[8,8,2,64]{3,2,0,1:T(2,128)S(1)} %collective-permute-done.28), channel_id=1, source_target_pairs={{0,32},{16,48},{32,0},{48,16},{1,33},{17,49},{33,1},{49,17},{2,34}... | collective-permute-start | bytes 98312 | tf_op jit(solution)/shard_map/ppermute | solution.py:23
  308.4 7.9 %collective-permute-start.7 = (f32[6,1,4,4,128]{4,2,1,0,3:T(4,128)S(1)}, f32[6,1,4,4,128]{4,2,1,0,3:T(4,128)S(1)}, u32[]{:S(2)}, u32[]{:S(2)}) collective-permute-start(f32[6,1,4,4,128]{4,2,1,0,3:T(4,128)S(1)} %collective-permute-done.6), channel_id=1, source_target_pairs={{0,16},{16,0},{32,48},{48,32},{1,17},{17,1},{33,49},{49,33},{2,18}... | collective-permute-start | bytes 147464 | tf_op jit(solution)/shard_map/ppermute | solution.py:23
  310.2 6.9 %collective-permute-start.11 = (f32[6,1,4,4,128]{4,2,1,0,3:T(4,128)S(1)}, f32[6,1,4,4,128]{4,2,1,0,3:T(4,128)S(1)}, u32[]{:S(2)}, u32[]{:S(2)}) collective-permute-start(f32[6,1,4,4,128]{4,2,1,0,3:T(4,128)S(1)} %collective-permute-done.10), channel_id=1, source_target_pairs={{0,128},{64,192},{128,0},{192,64},{1,129},{65,193},{129,1},{193,65... | collective-permute-start | bytes 147464 | tf_op jit(solution)/shard_map/ppermute | solution.py:23
  322.2 54.5 %collective-permute-start.12 = (f32[6,6,1,4,128]{4,2,1,0,3:T(1,128)S(1)}, f32[6,6,1,4,128]{4,2,1,0,3:T(1,128)S(1)}, u32[]{:S(2)}, u32[]{:S(2)}) collective-permute-start(f32[6,6,1,4,128]{4,2,1,0,3:T(1,128)S(1)} %get-tuple-element.983), channel_id=1, source_target_pairs={{0,4},{1,5},{2,6},{3,7},{4,0},{5,1},{6,2},{7,3},{8,12},{9,13},{10,... | collective-permute-start | bytes 221192 | tf_op jit(solution)/shard_map/ppermute | solution.py:23
  323.8 66.1 %collective-permute-start.14 = (f32[6,6,1,4,128]{4,2,1,0,3:T(1,128)S(1)}, f32[6,6,1,4,128]{4,2,1,0,3:T(1,128)S(1)}, u32[]{:S(2)}, u32[]{:S(2)}) collective-permute-start(f32[6,6,1,4,128]{4,2,1,0,3:T(1,128)S(1)} %get-tuple-element.984), channel_id=1, source_target_pairs={{0,4},{1,5},{2,6},{3,7},{4,0},{5,1},{6,2},{7,3},{8,12},{9,13},{10,... | collective-permute-start | bytes 221192 | tf_op jit(solution)/shard_map/ppermute | solution.py:23
  376.7 14.1 %collective-permute-start.13 = (f32[6,6,1,4,128]{4,2,1,0,3:T(1,128)S(1)}, f32[6,6,1,4,128]{4,2,1,0,3:T(1,128)S(1)}, u32[]{:S(2)}, u32[]{:S(2)}) collective-permute-start(f32[6,6,1,4,128]{4,2,1,0,3:T(1,128)S(1)} %collective-permute-done.12), channel_id=1, source_target_pairs={{0,32},{16,48},{32,0},{48,16},{1,33},{17,49},{33,1},{49,17},{2,34}... | collective-permute-start | bytes 221192 | tf_op jit(solution)/shard_map/ppermute | solution.py:23
  389.9 6.1 %collective-permute-start.15 = (f32[6,6,1,4,128]{4,2,1,0,3:T(1,128)S(1)}, f32[6,6,1,4,128]{4,2,1,0,3:T(1,128)S(1)}, u32[]{:S(2)}, u32[]{:S(2)}) collective-permute-start(f32[6,6,1,4,128]{4,2,1,0,3:T(1,128)S(1)} %collective-permute-done.14), channel_id=1, source_target_pairs={{0,32},{16,48},{32,0},{48,16},{1,33},{17,49},{33,1},{49,17},{2,34}... | collective-permute-start | bytes 221192 | tf_op jit(solution)/shard_map/ppermute | solution.py:23
  (25 other events, 354.1 us)
where the time goes:
time: 592 us; the launch traced here: 583 us
  matrix products  318 us (54%)
  local copies, waits for them, and re-layouts  115 us (19%)
  starting transfers between devices  51.8 us (9%)
  other arithmetic  47 us (8%)
  waiting for transfers between devices  25 us (4%)
  loops' own time  24.9 us (4%)
    dot_general x27, matrix products, pair_potential(): jnp.einsum('nts,ns->nt', weight, source[:, 3, :], precision=EXACT_DOTS)  277 us
    and x343, local copies, waits for them, and re-layouts, over_x(): okay_x[:, None, None] & okay_y[None, :, None] & okay_z[None, None, :]  74.2 us
    ppermute x32, starting transfers between devices, from_partner(): return lax.ppermute(value, axis, pairs)  51.8 us
    dot_general x7, matrix products, over_x(): jnp.einsum('oxyzj,oij->xyzi', weighted, jnp.stack(matrices), precision=EX...  34.3 us
    while x336, other arithmetic  33.6 us
    ppermute x32, waiting for transfers between devices, from_partner(): return lax.ppermute(value, axis, pairs)  25 us
    another operation x1, loops' own time, translate(): result, _ = lax.scan(over_x, start, jnp.arange(-3, 4, dtype=jnp.int32))  24.9 us
    while x350, local copies, waits for them, and re-layouts  16.9 us
  transfers between devices with their start and end apart: 32, of which 10 were waited for; matrix products, arithmetic and copies ran while one was open for 48% of the time, Pallas kernels for 0%

commit v1 on v0

v1 whole, which is shorter than its diff:
```python
import jax
import jax.numpy as jnp
from jax import lax
from jax.experimental import pallas as pl
from jax.experimental.pallas import tpu as pltpu
from jax.sharding import PartitionSpec as P

SOFTEN = 0.0025
HIGH = lax.Precision.HIGHEST
AXES = ("gx", "gy", "gz")
BITS = ((0, 3, 6), (1, 4, 7), (2, 5))
EXTENT = (8, 8, 4)
F32 = jnp.float32
BF16 = jnp.bfloat16
VMEM = pltpu.VMEM
SMEM = pltpu.SMEM
X_ROWS = 88
Y_ROWS = 136
Z_ROWS = 224


def place(q):
    return [sum(((q >> b) & 1) << k for k, b in enumerate(BITS[d])) for d in range(3)]


def linear(c):
    return sum(((c[d] >> k) & 1) << b for d in range(3) for k, b in enumerate(BITS[d]))


def shifted(dimension, step):
    pairs = []
    for q in range(256):
        c = place(q)
        c[dimension] = (c[dimension] + step) % EXTENT[dimension]
        pairs.append((q, linear(c)))
    return pairs


def lanes(shape):
    return lax.broadcasted_iota(jnp.int32, shape, len(shape) - 1)


def point_rows(pos, n):
    return jnp.concatenate([pos[d, pl.ds(n, 1), :] for d in range(3)], axis=0)


def dot(a, b):
    return jnp.dot(a, b, precision=HIGH, preferred_element_type=F32)


def upward_kernel(counts, pos, charges, outer, up_inv, own, xup, xdn, outer_b, source, density):
    oc = jnp.transpose(jnp.concatenate([outer[...], jnp.zeros((5, 64), F32)], axis=0))
    for d in range(3):
        outer_b[d] = jnp.broadcast_to(oc[:, d : d + 1], (64, 128))
    lane = lanes((1, 128))
    lane8 = lanes((64, 128))

    def one(n, check):
        p = point_rows(pos, n)
        q = jnp.where(lane < counts[n], charges[pl.ds(n, 1), :], 0.0)
        source[pl.ds(n, 1), :] = q
        square = SOFTEN
        for d in range(3):
            spread = outer_b[d] - p[d : d + 1]
            square = square + spread * spread
        col = jnp.sum(lax.rsqrt(square) * q, axis=1, keepdims=True)
        return jnp.where(lane8 == n, col, check)

    check = lax.fori_loop(0, 64, one, jnp.zeros((64, 128), F32), unroll=4)
    dens = dot(up_inv[...], check)
    density[...] = jnp.transpose(jnp.concatenate([dens, jnp.zeros((64, 128), F32)], axis=0))
    for hz in range(2):
        even = density[pl.ds(2 * hz, 16, stride=4), :]
        odd = density[pl.ds(2 * hz + 1, 16, stride=4), :]
        own[pl.ds(16 * hz, 16), :] = jnp.where(lane < 64, even, pltpu.roll(odd, 64, 1))
    for msg, x, xl in ((xup, 3, 2), (xdn, 0, 0)):
        for hz in range(2):
            msg[pl.ds(8 * hz, 8), :] = own[pl.ds(16 * hz + 4 * xl, 8), :]
        row = jnp.zeros((1, 128), F32)
        for k in range(16):
            n = 16 * x + k
            msg[pl.ds(16 + 4 * k, 3), :] = point_rows(pos, n)
            msg[pl.ds(16 + 4 * k + 3, 1), :] = source[pl.ds(n, 1), :]
            row = jnp.where(lane == k, counts[n].astype(F32), row)
        msg[pl.ds(80, 8), :] = jnp.broadcast_to(row, (8, 128))


def upward(counts, pos, charges, outer, up_inv):
    return pl.pallas_call(
        upward_kernel,
        out_shape=(
            jax.ShapeDtypeStruct((32, 128), F32),
            jax.ShapeDtypeStruct((X_ROWS, 128), F32),
            jax.ShapeDtypeStruct((X_ROWS, 128), F32),
        ),
        in_specs=[pl.BlockSpec(memory_space=SMEM)] + [pl.BlockSpec(memory_space=VMEM)] * 4,
        scratch_shapes=[VMEM((3, 64, 128), F32), VMEM((64, 128), F32), VMEM((128, 128), F32)],
        name="upward",
    )(counts, pos, charges, outer, up_inv)


def own_points(msg, at, pos, charges, counts, n):
    msg[pl.ds(at, 3), :] = point_rows(pos, n)
    msg[pl.ds(at + 3, 1), :] = jnp.where(lanes((1, 128)) < counts[n], charges[pl.ds(n, 1), :], 0.0)


def pack_y_kernel(counts, pos, charges, own, xlo, xhi, near, yup, ydn):
    lane = lanes((1, 128))
    row = jnp.zeros((1, 128), F32)
    for k in range(64):
        row = jnp.where(lane == k, counts[k].astype(F32), row)
    for msg, y, yl in ((yup, 3, 2), (ydn, 0, 0)):
        for hz in range(2):
            for ex in range(8):
                at = pl.ds((hz * 8 + ex) * 2, 2)
                if ex < 2:
                    msg[at, :] = xlo[pl.ds((hz * 2 + ex) * 4 + yl, 2), :]
                elif ex < 6:
                    msg[at, :] = own[pl.ds((hz * 4 + ex - 2) * 4 + yl, 2), :]
                else:
                    msg[at, :] = xhi[pl.ds((hz * 2 + ex - 6) * 4 + yl, 2), :]
        for z in range(4):
            msg[pl.ds(32 + 4 * z, 4), :] = xlo[pl.ds(16 + 4 * (4 * y + z), 4), :]
            for x in range(4):
                own_points(msg, 32 + 4 * (4 * (x + 1) + z), pos, charges, counts, 16 * x + 4 * y + z)
            msg[pl.ds(32 + 4 * (20 + z), 4), :] = xhi[pl.ds(16 + 4 * (4 * y + z), 4), :]
        msg[pl.ds(128, 1), :] = row
        msg[pl.ds(129, 1), :] = xlo[pl.ds(80, 1), :]
        msg[pl.ds(130, 1), :] = xhi[pl.ds(80, 1), :]
        msg[pl.ds(131, 5), :] = jnp.zeros((5, 128), F32)


def pack_y(counts, pos, charges, own, xlo, xhi, near):
    return pl.pallas_call(
        pack_y_kernel,
        out_shape=(jax.ShapeDtypeStruct((Y_ROWS, 128), F32),) * 2,
        in_specs=[pl.BlockSpec(memory_space=SMEM)] + [pl.BlockSpec(memory_space=VMEM)] * 5 + [pl.BlockSpec(memory_space=pl.ANY)],
        name="pack_y",
    )(counts, pos, charges, own, xlo, xhi, near)


def pack_z_kernel(counts, pos, charges, own, xlo, xhi, yup, ylo, yhi, near, zup, zdn):
    for msg, z, hz in ((zup, 3, 1), (zdn, 0, 0)):
        for ex in range(8):
            at = ex * 8
            msg[pl.ds(at, 2), :] = ylo[pl.ds((hz * 8 + ex) * 2, 2), :]
            if ex < 2:
                msg[pl.ds(at + 2, 4), :] = xlo[pl.ds((hz * 2 + ex) * 4, 4), :]
            elif ex < 6:
                msg[pl.ds(at + 2, 4), :] = own[pl.ds((hz * 4 + ex - 2) * 4, 4), :]
            else:
                msg[pl.ds(at + 2, 4), :] = xhi[pl.ds((hz * 2 + ex - 6) * 4, 4), :]
            msg[pl.ds(at + 6, 2), :] = yhi[pl.ds((hz * 8 + ex) * 2, 2), :]
        for ex in range(6):
            for ey in range(6):
                at = 64 + 4 * (6 * ex + ey)
                if ey == 0:
                    msg[pl.ds(at, 4), :] = ylo[pl.ds(32 + 4 * (4 * ex + z), 4), :]
                elif ey == 5:
                    msg[pl.ds(at, 4), :] = yhi[pl.ds(32 + 4 * (4 * ex + z), 4), :]
                elif ex == 0:
                    msg[pl.ds(at, 4), :] = xlo[pl.ds(16 + 4 * (4 * (ey - 1) + z), 4), :]
                elif ex == 5:
                    msg[pl.ds(at, 4), :] = xhi[pl.ds(16 + 4 * (4 * (ey - 1) + z), 4), :]
                else:
                    own_points(msg, at, pos, charges, counts, 16 * (ex - 1) + 4 * (ey - 1) + z)
        msg[pl.ds(208, 3), :] = yup[pl.ds(128, 3), :]
        msg[pl.ds(211, 3), :] = ylo[pl.ds(128, 3), :]
        msg[pl.ds(214, 3), :] = yhi[pl.ds(128, 3), :]
        msg[pl.ds(217, 7), :] = jnp.zeros((7, 128), F32)


def pack_z(counts, pos, charges, own, xlo, xhi, yup, ylo, yhi, near):
    return pl.pallas_call(
        pack_z_kernel,
        out_shape=(jax.ShapeDtypeStruct((Z_ROWS, 128), F32),) * 2,
        in_specs=[pl.BlockSpec(memory_space=SMEM)] + [pl.BlockSpec(memory_space=VMEM)] * 8 + [pl.BlockSpec(memory_space=pl.ANY)],
        name="pack_z",
    )(counts, pos, charges, own, xlo, xhi, yup, ylo, yhi, near)


def add_source(packed, base, place_at, leaf, count, cell, lane):
    off = jnp.bitwise_and(place_at, 127)
    tile = base + jnp.right_shift(place_at, 7)
    row = lax.broadcasted_iota(jnp.int32, (4, 128), 0)
    shift = jnp.where(row == 0, cell[0], jnp.where(row == 1, cell[1], jnp.where(row == 2, cell[2], 0.0)))
    rolled = pltpu.roll(leaf + shift, off, 1)
    packed[tile, pl.ds(0, 4), :] = jnp.where(lane >= off, rolled, packed[tile, pl.ds(0, 4), :])
    packed[tile + 1, pl.ds(0, 4), :] = rolled
    return place_at + count


def close_list(packed, base, end):
    packed[base + jnp.right_shift(end, 7) + 1, pl.ds(0, 4), :] = jnp.zeros((4, 128), F32)
    packed[base + jnp.right_shift(end, 7) + 2, pl.ds(0, 4), :] = jnp.zeros((4, 128), F32)


def cell_of(n):
    return jnp.right_shift(n, 4), jnp.bitwise_and(jnp.right_shift(n, 2), 3), jnp.bitwise_and(n, 3)


def spread_targets(pos, spread, leaf_of, leaves):
    row = lax.broadcasted_iota(jnp.int32, (8, 128), 0)

    def one(i, carry):
        n = leaf_of(i)
        x, y, z = [c.astype(F32) for c in cell_of(n)]
        shift = jnp.where(row == 0, x, jnp.where(row == 1, y, z))
        flat = jnp.concatenate([point_rows(pos, n), jnp.zeros((5, 128), F32)], axis=0) + shift
        turned = jnp.transpose(flat)
        for d in range(3):
            spread[i, d] = jnp.broadcast_to(turned[:, d : d + 1], (128, 128))
        return carry

    lax.fori_loop(0, leaves, one, 0, unroll=4)


def near_sums(i, count, spread, sums, packed, segments):
    lane = lanes((1, 128))
    tiles, starts, stops, upto = [], [], [], []
    have = jnp.int32(0)
    for base, start, stop in segments:
        first = jnp.right_shift(start, 7)
        number = jnp.where(stop > start, jnp.right_shift(stop + 127, 7) - first, 0)
        tiles.append(base + first - have)
        starts.append(base * 128 + start)
        stops.append(base * 128 + stop)
        have = have + number
        upto.append(have)

    def pick(values, j):
        value = values[-1]
        for k in range(len(values) - 2, -1, -1):
            value = jnp.where(j < upto[k], values[k], value)
        return value

    def run(groups, together):
        rows = pl.ds(0, 8 * groups)
        blocks = lax.div(have + together - 1, together)

        def ahead(b):
            squares, charges = [], []
            for u in range(together):
                j = b * together + u
                tile = pick(tiles, j) + jnp.minimum(j, have - 1)
                at = tile * 128 + lane
                keep = (at >= pick(starts, j)) & (at < jnp.where(j < have, pick(stops, j), 0))
                charges.append(jnp.where(keep, packed[tile, pl.ds(3, 1), :], 0.0))
                square = SOFTEN
                for d in range(3):
                    gap = spread[i, d, rows, :] - packed[tile, pl.ds(d, 1), :]
                    square = square + gap * gap
                squares.append(square)
            return squares, charges

        def add(acc, squares, charges):
            for square, charge in zip(squares, charges):
                acc = acc + lax.rsqrt(square) * charge
            return acc

        def step(b, carry):
            acc, squares, charges = carry
            later = ahead(b)
            return (add(acc, squares, charges), *later)

        acc, squares, charges = lax.fori_loop(
            1, blocks, step, (jnp.zeros((8 * groups, 128), F32), *ahead(0))
        )
        sums[i, rows, :] = add(acc, squares, charges)

    size = jnp.right_shift(count + 31, 5)
    for k, together in ((1, 4), (2, 2), (3, 1), (4, 1)):

        @pl.when(size == k)
        def _():
            run(4 * k, together)


def gather_sums(sums, total, leaf_of, leaves):
    wide = lanes((128, 128))

    def one(i, carry):
        col = jnp.sum(sums[i], axis=1, keepdims=True)
        return jnp.where(wide == leaf_of(i), carry + col, carry)

    total[...] = lax.fori_loop(0, leaves, one, total[...], unroll=4)


def near_xy_kernel(windows, *refs):
    if len(refs) == 9:
        counts, pos, charges, total, packed, spread, sums, ends, _ = refs
        xlo = xhi = None
    else:
        counts, flags, pos, charges, xlo, xhi, before, total, packed, spread, sums, ends, lo_counts, hi_counts, sem = refs
        a = pltpu.make_async_copy(xlo.at[pl.ds(80, 1), :], lo_counts, sem.at[0])
        b = pltpu.make_async_copy(xhi.at[pl.ds(80, 1), :], hi_counts, sem.at[1])
        a.start()
        b.start()
        a.wait()
        b.wait()
    lane4 = lanes((4, 128))
    lane = lanes((1, 128))
    total[...] = jnp.zeros((128, 128), F32) if xlo is None else before[...]
    for w, x in enumerate(windows):
        for z in range(4):
            base = (w * 4 + z) * 16
            end = jnp.int32(0)
            ends[(w * 4 + z) * 5] = end
            for y in range(4):
                for dx in (-1, 0, 1):
                    sx = x + dx
                    k = 4 * y + z
                    cell = (float(sx), float(y), float(z))
                    if 0 <= sx < 4:
                        n = 16 * sx + k
                        count = counts[n]
                        q = jnp.where(lane < count, charges[pl.ds(n, 1), :], 0.0)
                        leaf = jnp.concatenate([point_rows(pos, n), q], axis=0)
                    else:
                        msg, cnt, flag = (xlo, lo_counts, 0) if sx < 0 else (xhi, hi_counts, 1)
                        count = cnt[0, k].astype(jnp.int32) * flags[flag]
                        leaf = msg[pl.ds(16 + 4 * k, 4), :]
                    end = add_source(packed, base, end, leaf, count, cell, lane4)
                ends[(w * 4 + z) * 5 + y + 1] = end
            close_list(packed, base, end)

    def leaf_of(i):
        return jnp.bitwise_and(i, 15) + 16 * (windows[0] + jnp.right_shift(i, 4) * (windows[1] - windows[0]))

    spread_targets(pos, spread, leaf_of, 32)

    def leaf_step(i, carry):
        w = jnp.right_shift(i, 4)
        n = leaf_of(i)
        x, y, z = cell_of(n)
        segments = []
        for dz in (-1, 0, 1):
            zz = jnp.clip(z + dz, 0, 3)
            lst = w * 4 + zz
            start = ends[lst * 5 + jnp.maximum(y - 1, 0)]
            stop = ends[lst * 5 + jnp.minimum(y + 1, 3) + 1]
            if dz:
                stop = jnp.where(zz == z + dz, stop, start)
            segments.append((lst * 16, start, stop))
        near_sums(i, counts[n], spread, sums, packed, segments)
        return carry

    lax.fori_loop(0, 32, leaf_step, 0)
    gather_sums(sums, total, leaf_of, 32)


def near_xy(windows, counts, pos, charges, halo=None):
    call_args = [counts, pos, charges]
    specs = [pl.BlockSpec(memory_space=SMEM)] + [pl.BlockSpec(memory_space=VMEM)] * 2
    if halo is not None:
        flags, xlo, xhi, before = halo
        call_args = [counts, flags, pos, charges, xlo, xhi, before]
        specs = [pl.BlockSpec(memory_space=SMEM)] * 2 + [pl.BlockSpec(memory_space=VMEM)] * 5
    scratch = [
        VMEM((8 * 16, 8, 128), F32),
        VMEM((32, 3, 128, 128), F32),
        VMEM((32, 128, 128), F32),
        SMEM((40,), jnp.int32),
        SMEM((1, 128), F32),
    ]
    if halo is not None:
        scratch += [SMEM((1, 128), F32), pltpu.SemaphoreType.DMA((2,))]

    def body(*refs):
        near_xy_kernel(windows, *refs)

    return pl.pallas_call(
        body,
        out_shape=jax.ShapeDtypeStruct((128, 128), F32),
        in_specs=specs,
        scratch_shapes=scratch,
        compiler_params=pltpu.CompilerParams(vmem_limit_bytes=24 * 1024 * 1024),
        cost_estimate=pl.CostEstimate(flops=150_000_000, bytes_accessed=300_000, transcendentals=10_000_000),
        name="near_x",
    )(*call_args)


def near_y_kernel(counts, flags, pos, ylo, yhi, before, total, packed, spread, sums, ends, row_counts, sem):
    copies = [
        pltpu.make_async_copy(msg.at[pl.ds(128, 8), :], row_counts.at[i], sem.at[i])
        for i, msg in enumerate((ylo, yhi))
    ]
    for c in copies:
        c.start()
    for c in copies:
        c.wait()
    lane4 = lanes((4, 128))
    total[...] = before[...]
    for side, msg in enumerate((ylo, yhi)):
        sy = -1 if side == 0 else 4
        far_y = 3 if side == 0 else 0
        for z in range(4):
            lst = side * 4 + z
            end = jnp.int32(0)
            ends[lst * 7] = end
            for ex in range(6):
                if ex == 0:
                    count = row_counts[side, 1, 4 * far_y + z].astype(jnp.int32) * flags[0]
                elif ex == 5:
                    count = row_counts[side, 2, 4 * far_y + z].astype(jnp.int32) * flags[1]
                else:
                    count = row_counts[side, 0, 16 * (ex - 1) + 4 * far_y + z].astype(jnp.int32)
                count = count * flags[2 + side]
                leaf = msg[pl.ds(32 + 4 * (4 * ex + z), 4), :]
                end = add_source(packed, lst * 10, end, leaf, count, (float(ex - 1), float(sy), float(z)), lane4)
                ends[lst * 7 + ex + 1] = end
            close_list(packed, lst * 10, end)

    def leaf_of(i):
        side = jnp.right_shift(i, 4)
        x = jnp.bitwise_and(jnp.right_shift(i, 2), 3)
        return 16 * x + 12 * side + jnp.bitwise_and(i, 3)

    spread_targets(pos, spread, leaf_of, 32)

    def leaf_step(i, carry):
        side = jnp.right_shift(i, 4)
        n = leaf_of(i)
        x, y, z = cell_of(n)
        segments = []
        for dz in (-1, 0, 1):
            zz = jnp.clip(z + dz, 0, 3)
            lst = side * 4 + zz
            start = ends[lst * 7 + x]
            stop = ends[lst * 7 + x + 3]
            if dz:
                stop = jnp.where(zz == z + dz, stop, start)
            segments.append((lst * 10, start, stop))
        near_sums(i, counts[n], spread, sums, packed, segments)
        return carry

    lax.fori_loop(0, 32, leaf_step, 0)
    gather_sums(sums, total, leaf_of, 32)


def near_y(counts, flags, pos, ylo, yhi, before):
    return pl.pallas_call(
        near_y_kernel,
        out_shape=jax.ShapeDtypeStruct((128, 128), F32),
        in_specs=[pl.BlockSpec(memory_space=SMEM)] * 2 + [pl.BlockSpec(memory_space=VMEM)] * 4,
        scratch_shapes=[
            VMEM((8 * 10, 8, 128), F32),
            VMEM((32, 3, 128, 128), F32),
            VMEM((32, 128, 128), F32),
            SMEM((56,), jnp.int32),
            SMEM((2, 8, 128), F32),
            pltpu.SemaphoreType.DMA((2,)),
        ],
        compiler_params=pltpu.CompilerParams(vmem_limit_bytes=24 * 1024 * 1024),
        cost_estimate=pl.CostEstimate(flops=60_000_000, bytes_accessed=300_000, transcendentals=4_000_000),
        name="near_y",
    )(counts, flags, pos, ylo, yhi, before)


def final_kernel(
    counts, flags, pos, charges, zup, zdn, zlo, zhi, before, inner, outer, down_inv,
    out, packed, spread, sums, ends, row_counts, total, grid, weights, left, local, sem,
):
    copies = [
        pltpu.make_async_copy(msg.at[pl.ds(208, 16), :], row_counts.at[i], sem.at[i])
        for i, msg in enumerate((zlo, zhi))
    ]
    for c in copies:
        c.start()
    grid[1] = zdn[pl.ds(0, 64), :].reshape(8, 8, 128)
    grid[2] = zup[pl.ds(0, 64), :].reshape(8, 8, 128)
    grid[0] = zlo[pl.ds(0, 64), :].reshape(8, 8, 128)
    grid[3] = zhi[pl.ds(0, 64), :].reshape(8, 8, 128)

    @pl.when(flags[0] == 0)
    def _():
        grid[:, pl.ds(0, 2)] = jnp.zeros((4, 2, 8, 128), F32)

    @pl.when(flags[1] == 0)
    def _():
        grid[:, pl.ds(6, 2)] = jnp.zeros((4, 2, 8, 128), F32)

    @pl.when(flags[2] == 0)
    def _():
        grid[:, :, pl.ds(0, 2), :] = jnp.zeros((4, 8, 2, 128), F32)

    @pl.when(flags[3] == 0)
    def _():
        grid[:, :, pl.ds(6, 2), :] = jnp.zeros((4, 8, 2, 128), F32)

    @pl.when(flags[4] == 0)
    def _():
        grid[0] = jnp.zeros((8, 8, 128), F32)

    @pl.when(flags[5] == 0)
    def _():
        grid[3] = jnp.zeros((8, 8, 128), F32)

    odd_row = jnp.bitwise_and(lax.broadcasted_iota(jnp.int32, (8, 128), 0), 1) == 1
    for oy in range(7):
        for x in range(8):
            for hb in range(3):
                begin = min(max(oy - 1, 0), 4)
                both = jnp.concatenate(
                    [grid[hb, x, pl.ds(begin, 4), :], grid[hb + 1, x, pl.ds(begin, 4), :]], axis=0
                )
                if oy == 0:
                    both = jnp.where(odd_row, pltpu.roll(both, 1, 0), 0.0)
                elif oy == 6:
                    both = jnp.where(odd_row, 0.0, pltpu.roll(both, 7, 0))
                first = both.astype(BF16)
                left[0, x, :, pl.ds(oy * 384 + hb * 128, 128)] = first.astype(F32)
                left[1, x, :, pl.ds(oy * 384 + hb * 128, 128)] = both - first.astype(F32)

    inner_rows = jnp.concatenate([inner[...], jnp.zeros((5, 64), F32)], axis=0)
    inner_cols = jnp.transpose(inner_rows)
    diff = [
        jnp.concatenate([inner[d : d + 1, :], inner[d : d + 1, :]], axis=1) - jnp.broadcast_to(inner_cols[:, d : d + 1], (64, 128))
        for d in range(3)
    ]
    wide = lanes((64, 128))
    right = jnp.where(wide >= 64, 1.0, 0.0)
    zsq = []
    for sz in range(6):
        offset = float(sz - 2) - right
        gap = diff[2] - offset
        zsq.append(gap * gap + SOFTEN)
    check = [None] * 4

    def over_x(ox, xs, rows):
        gap_x = diff[0] - float(ox)
        xsq = gap_x * gap_x
        for oy in range(-3, 4):
            gap_y = diff[1] - float(oy)
            xysq = xsq + gap_y * gap_y
            for sz in range(6):
                value = lax.rsqrt(xysq + zsq[sz])
                if max(abs(ox), abs(oy)) < 2:
                    left_near = abs(sz - 2) < 2
                    right_near = abs(sz - 3) < 2
                    if left_near:
                        value = jnp.where(wide < 64, 0.0, value)
                    if right_near:
                        value = jnp.where(wide >= 64, 0.0, value)
                first = value.astype(BF16)
                at = pl.ds((oy + 3) * 384 + sz * 64, 64)
                weights[at, pl.ds(0, 128)] = first
                weights[at, pl.ds(128, 128)] = (value - first.astype(F32)).astype(BF16)
        m = 8 * len(xs)
        lhs = jnp.concatenate([left[p, x] for p in range(2) for x in rows], axis=0).astype(BF16)
        prod = jnp.dot(lhs, weights[...], preferred_element_type=F32)
        part = prod[:m, :128] + prod[:m, 128:] + prod[m:, :128]
        for i, x in enumerate(xs):
            piece = part[8 * i : 8 * i + 8]
            check[x] = piece if check[x] is None else check[x] + piece

    for ox in range(-3, 4):
        if ox == -3:
            xs = (1, 3)
        elif ox == 3:
            xs = (0, 2)
        else:
            xs = (0, 1, 2, 3)
        over_x(ox, xs, [x + ox + 2 for x in xs])
    down = check_to_local(jnp.concatenate(check, axis=0), down_inv)
    local[...] = down

    for c in copies:
        c.wait()
    lane4 = lanes((4, 128))
    total[...] = before[...]
    for side, msg in enumerate((zlo, zhi)):
        sz = -1 if side == 0 else 4
        far_z = 3 if side == 0 else 0
        for ey in range(6):
            lst = side * 6 + ey
            end = jnp.int32(0)
            ends[lst * 7] = end
            for ex in range(6):
                group = 3 if ey == 0 else (6 if ey == 5 else 0)
                y = 3 if ey == 0 else (0 if ey == 5 else ey - 1)
                if ex == 0:
                    count = row_counts[side, group + 1, 4 * y + far_z].astype(jnp.int32) * flags[0]
                elif ex == 5:
                    count = row_counts[side, group + 2, 4 * y + far_z].astype(jnp.int32) * flags[1]
                else:
                    count = row_counts[side, group, 16 * (ex - 1) + 4 * y + far_z].astype(jnp.int32)
                if ey == 0:
                    count = count * flags[2]
                elif ey == 5:
                    count = count * flags[3]
                count = count * flags[4 + side]
                leaf = msg[pl.ds(64 + 4 * (6 * ex + ey), 4), :]
                end = add_source(packed, lst * 10, end, leaf, count, (float(ex - 1), float(ey - 1), float(sz)), lane4)
                ends[lst * 7 + ex + 1] = end
            close_list(packed, lst * 10, end)

    outer_twice = jnp.concatenate([outer[...], outer[...]], axis=1)
    lane = lanes((1, 128))

    def far_source(n, carry):
        x, y, z = cell_of(n)
        for d, c in enumerate((x, y, z)):
            packed[120 + n, pl.ds(d, 1), :] = outer_twice[d : d + 1] + c.astype(F32)
        weight = local[pl.ds(x * 8 + jnp.right_shift(z, 1) * 4 + y, 1), :]
        mine = jnp.right_shift(lane, 6) == jnp.bitwise_and(z, 1)
        packed[120 + n, pl.ds(3, 1), :] = jnp.where(mine, weight, 0.0)
        return carry

    lax.fori_loop(0, 64, far_source, 0, unroll=8)
    spread_targets(pos, spread, lambda i: i, 64)

    def leaf_step(n, carry):
        x, y, z = cell_of(n)
        side = jnp.right_shift(z, 1)
        edge = (z == 0) | (z == 3)
        segments = [(120 + n, jnp.int32(0), jnp.int32(128))]
        for dy in range(3):
            lst = side * 6 + y + dy
            start = ends[lst * 7 + x]
            stop = jnp.where(edge, ends[lst * 7 + x + 3], start)
            segments.append((lst * 10, start, stop))
        near_sums(n, counts[n], spread, sums, packed, segments)
        return carry

    lax.fori_loop(0, 64, leaf_step, 0)
    gather_sums(sums, total, lambda i: i, 64)
    both = jnp.transpose(total[...])
    row = lax.broadcasted_iota(jnp.int32, (64, 1), 0)
    full = jnp.zeros((64, 1), jnp.int32)
    for n in range(64):
        full = jnp.where(row == n, counts[n], full)
    live = lanes((64, 128)) < full
    own_term = lax.rsqrt(jnp.full((64, 128), SOFTEN, F32))
    out[...] = jnp.where(live, both[:64] - own_term * charges[...], 0.0)


def check_to_local(check, down_inv):
    flat = jnp.transpose(down_inv[...])
    zero = jnp.zeros((64, 64), F32)
    block = jnp.concatenate(
        [jnp.concatenate([flat, zero], axis=1), jnp.concatenate([zero, flat], axis=1)], axis=0
    )
    return dot(check, block)


def final(counts, flags, pos, charges, zup, zdn, zlo, zhi, before, inner, outer, down_inv):
    return pl.pallas_call(
        final_kernel,
        out_shape=jax.ShapeDtypeStruct((64, 128), F32),
        in_specs=[pl.BlockSpec(memory_space=SMEM)] * 2 + [pl.BlockSpec(memory_space=VMEM)] * 10,
        scratch_shapes=[
            VMEM((12 * 10 + 64, 8, 128), F32),
            VMEM((64, 3, 128, 128), F32),
            VMEM((64, 128, 128), F32),
            SMEM((84,), jnp.int32),
            SMEM((2, 16, 128), F32),
            VMEM((128, 128), F32),
            VMEM((4, 8, 8, 128), F32),
            VMEM((2688, 256), BF16),
            VMEM((2, 8, 8, 2688), F32),
            VMEM((32, 128), F32),
            pltpu.SemaphoreType.DMA((2,)),
        ],
        compiler_params=pltpu.CompilerParams(vmem_limit_bytes=56 * 1024 * 1024),
        name="final",
    )(counts, flags, pos, charges, zup, zdn, zlo, zhi, before, inner, outer, down_inv)


def exchange(up, down, dimension):
    return (
        lax.ppermute(up, AXES, shifted(dimension, 1)),
        lax.ppermute(down, AXES, shifted(dimension, -1)),
    )


def per_device(positions, charges, counts, up_inverse, down_inverse, inner_surface, outer_surface):
    device = (lax.axis_index("gx") * 4 + lax.axis_index("gy")) * 16 + lax.axis_index("gz")
    sides = []
    for d in range(3):
        at = jnp.zeros((), jnp.int32)
        for k, b in enumerate(BITS[d]):
            at = at + jnp.left_shift(jnp.bitwise_and(jnp.right_shift(device, b), 1), k)
        sides += [at > 0, at < EXTENT[d] - 1]
    flags = jnp.stack(sides).astype(jnp.int32)
    positions = jnp.transpose(positions, (1, 0, 2))
    own, xup, xdn = upward(counts, positions, charges, outer_surface, up_inverse)
    xlo, xhi = exchange(xup, xdn, 0)
    near = near_xy((1, 2), counts, positions, charges)
    yup, ydn = pack_y(counts, positions, charges, own, xlo, xhi, near)
    ylo, yhi = exchange(yup, ydn, 1)
    near = near_xy((0, 3), counts, positions, charges, (flags, xlo, xhi, near))
    zup, zdn = pack_z(counts, positions, charges, own, xlo, xhi, yup, ylo, yhi, near)
    zlo, zhi = exchange(zup, zdn, 2)
    near = near_y(counts, flags, positions, ylo, yhi, near)
    return final(
        counts, flags, positions, charges, zup, zdn, zlo, zhi, near, inner_surface, outer_surface, down_inverse
    )


def solution(mesh):
    split = AXES
    return jax.shard_map(
        per_device,
        mesh=mesh,
        in_specs=(P(split, None, None), P(split, None), P(split), P(), P(), P(), P()),
        out_specs=P(split, None),
        check_vma=False,
    )
```

time: 592 us -> 114 us (0.19)
  the two profiles are of different devices: /device:TPU:16 before, /device:TPU:184 now
where the time goes in v1:
time: 114 us; the launch traced here: 112 us
  Pallas kernels  86.8 us (76%)
  starting transfers between devices  16.3 us (14%)
  local copies, waits for them, and re-layouts  9.07 us (8%)
    pallas_call x2, Pallas kernels, near_xy(): pl.pallas_call(body, out_shape=jax.ShapeDtypeStruct((128, 128), F32), in_...  36.6 us
    pallas_call x1, Pallas kernels, final(): pl.pallas_call(final_kernel, out_shape=jax.ShapeDtypeStruct((64, 128), F3...  28.7 us
    pallas_call x1, Pallas kernels, near_y(): pl.pallas_call(near_y_kernel, out_shape=jax.ShapeDtypeStruct((128, 128),...  13.5 us
    ppermute x3, starting transfers between devices, exchange(): lax.ppermute(down, AXES, shifted(dimension, -1))  11 us
    unnamed x48, local copies, waits for them, and re-layouts  8.97 us
    ppermute x3, starting transfers between devices, exchange(): lax.ppermute(up, AXES, shifted(dimension, 1))  5.32 us
    pallas_call x1, Pallas kernels, upward(): pl.pallas_call(upward_kernel, out_shape=(jax.ShapeDtypeStruct((32, 128),...  4.38 us
  transfers between devices with their start and end apart: 6, of which 0 were waited for; matrix products, arithmetic and copies ran while one was open for 0% of the time, Pallas kernels for 45%

profile of v1, /device:TPU:184, one launch (start us, length us, event | category | flops | bytes accessed | tf_op | source)
XLA Modules:
  0.0 112.4 jit_solution(2165819262744126422)
XLA Ops:
  0.0 4.4 %upward.1 = (f32[32,128]{1,0:T(8,128)}, f32[88,128]{1,0:T(8,128)}, f32[88,128]{1,0:T(8,128)}) custom-call(s32[64]{0:T(128)} %counts.9, f32[3,64,128]{2,1,0:T(8,128)} %bitcast.7, f32[64,128]{1,0:T(8,128)} %charges.7, f32[3,64]{1,0:T(4,128)} %outer.3, f32[64,64]{1,0:T(8,128)} %up_inv.1), custom_call_target="tpu_custom_call" | custom-call | tf_op jit(solution)/shard_map/upward/pallas_call | solution.py:89
  4.4 5.7 %collective-permute-start.1 = (f32[88,128]{1,0:T(8,128)}, f32[88,128]{1,0:T(8,128)S(1)}, u32[]{:S(2)}, u32[]{:S(2)}) collective-permute-start(f32[88,128]{1,0:T(8,128)} %get-tuple-element.14), channel_id=1, source_target_pairs={{0,73},{1,0},{2,75},{3,2},{4,77},{5,4},{6,79},{7,6},{8,1},{9,8},{1... | collective-permute-start | bytes 135176 | tf_op jit(solution)/shard_map/ppermute | solution.py:673
  10.0 18.8 %near_x.2.near.refs_6_ = f32[128,128]{1,0:T(8,128)S(1)} custom-call(s32[64]{0:T(128)S(1)} %copy-done.18, f32[3,64,128]{2,1,0:T(8,128)S(1)} %bitcast.11, f32[64,128]{1,0:T(8,128)S(1)} %copy-done.3), custom_call_target="tpu_custom_call" | custom-call | flops 150000000 | bytes 300000 | tf_op jit(solution)/shard_map/near_x/pallas_call | solution.py:372
  28.8 0.6 copy-done.13
  29.4 0.6 copy-done.5
  30.1 1.7 %pack_y.1 = (f32[136,128]{1,0:T(8,128)}, f32[136,128]{1,0:T(8,128)}) custom-call(s32[64]{0:T(128)} %counts.9, f32[3,64,128]{2,1,0:T(8,128)} %bitcast.8, f32[64,128]{1,0:T(8,128)} %charges.7, f32[32,128]{1,0:T(8,128)} %get-tuple-element.12.own, f32[88,128]{1,0:T(8,128)} %copy-done.5, f32[88,128]{1,0:T(8,128)} %copy-done.7, f32[128,128]{1,0:T(8,128)} %copy-done.13), custom_call_target="tpu_custom_call" | custom-call | tf_op jit(solution)/shard_map/pack_y/pallas_call | solution.py:134
  31.8 0.2 collective-permute-start.3
  32.0 5.1 %collective-permute-start.2 = (f32[136,128]{1,0:T(8,128)}, f32[136,128]{1,0:T(8,128)S(1)}, u32[]{:S(2)}, u32[]{:S(2)}) collective-permute-start(f32[136,128]{1,0:T(8,128)} %get-tuple-element.15.yup), channel_id=1, source_target_pairs={{0,2},{1,3},{2,16},{3,17},{4,6},{5,7},{6,20},{7,21},{8,10},{9,11},... | collective-permute-start | bytes 208904 | tf_op jit(solution)/shard_map/ppermute | solution.py:672
  37.3 0.6 copy-done.19
  37.9 0.8 copy-done.6
  38.7 0.8 copy-done.8
  39.5 17.8 %near_x.3.near.before = f32[128,128]{1,0:T(8,128)S(1)} custom-call(s32[64]{0:T(128)S(1)} %copy-done.19, s32[6]{0:T(128)S(1)} %convert_element_type.3.refs_1_.flags, f32[3,64,128]{2,1,0:T(8,128)S(1)} %bitcast.12, f32[64,128]{1,0:T(8,128)S(1)} %copy-done.4, f32[88,128]{1,0:T(8,128)S(1)} %copy-done.6, f32[88,128]{1,0:T(8,128)S(1)} %copy-done.8, ...), custom_call_target="tpu_custom_call" | custom-call | flops 150000000 | bytes 300000 | tf_op jit(solution)/shard_map/near_x/pallas_call | solution.py:372
  57.3 0.6 copy-done.15
  57.9 0.6 copy-done.9
  58.6 0.6 copy-done.11
  59.2 1.9 %pack_z.1 = (f32[224,128]{1,0:T(8,128)}, f32[224,128]{1,0:T(8,128)}) custom-call(s32[64]{0:T(128)} %counts.9, f32[3,64,128]{2,1,0:T(8,128)} %bitcast.9, f32[64,128]{1,0:T(8,128)} %charges.7, f32[32,128]{1,0:T(8,128)} %get-tuple-element.12.own, f32[88,128]{1,0:T(8,128)} %copy-done.5, f32[88,128]{1,0:T(8,128)} %copy-done.7, f32[136,128]{1,0:T(8,128)} %get-tuple-element.15.yup, ...), custom_call_target="tpu_custom_call" | custom-call | tf_op jit(solution)/shard_map/pack_z/pallas_call | solution.py:174
  61.3 5.1 %collective-permute-start.5 = (f32[224,128]{1,0:T(8,128)}, f32[224,128]{1,0:T(8,128)S(1)}, u32[]{:S(2)}, u32[]{:S(2)}) collective-permute-start(f32[224,128]{1,0:T(8,128)} %get-tuple-element.18.zdn), channel_id=1, source_target_pairs={{0,36},{1,37},{2,38},{3,39},{4,0},{5,1},{6,2},{7,3},{8,44},{9,45},... | collective-permute-start | bytes 344072 | tf_op jit(solution)/shard_map/ppermute | solution.py:673
  66.4 0.9 copy-done.10
  67.3 0.9 copy-done.12
  68.2 13.5 %near_y.1.before = f32[128,128]{1,0:T(8,128)S(1)} custom-call(s32[64]{0:T(128)S(1)} %copy-done.20, s32[6]{0:T(128)S(1)} %convert_element_type.3.refs_1_.flags, f32[3,64,128]{2,1,0:T(8,128)S(1)} %bitcast.13, f32[136,128]{1,0:T(8,128)S(1)} %copy-done.12, f32[136,128]{1,0:T(8,128)S(1)} %copy-done.10, f32[128,128]{1,0:T(8,128)S(1)} %copy-done.16), custom_call_target="tpu_custom_call" | custom-call | flops 60000000 | bytes 300000 | tf_op jit(solution)/shard_map/near_y/pallas_call | solution.py:442
  81.7 0.6 copy-done.17
  82.3 0.6 copy-done.22
  83.0 0.6 copy-done.23
  83.6 28.7 %final.1 = f32[64,128]{1,0:T(8,128)} custom-call(s32[64]{0:T(128)} %counts.9, s32[6]{0:T(128)} %copy-done.21, f32[3,64,128]{2,1,0:T(8,128)} %bitcast.10, f32[64,128]{1,0:T(8,128)} %charges.7, f32[224,128]{1,0:T(8,128)} %get-tuple-element.17.zup, f32[224,128]{1,0:T(8,128)} %get-tuple-element.18.zdn, f32[224,128]{1,0:T(8,128)} %copy-done.22, ...), custom_call_target="tpu_custom_call" | custom-call | tf_op jit(solution)/shard_map/final/pallas_call | solution.py:648
  (45 shorter events, 0.4 us)
Async XLA Ops:
  0.0 10.0 %copy-start = (f32[64,3,128]{2,0,1:T(8,128)S(1)}, f32[64,3,128]{2,0,1:T(8,128)}, u32[]{:S(2)}) copy-start(f32[64,3,128]{2,0,1:T(8,128)} %param.7) | copy-start | bytes 294916
  0.0 10.0 %copy-start.3 = (f32[64,128]{1,0:T(8,128)S(1)}, f32[64,128]{1,0:T(8,128)}, u32[]{:S(2)}) copy-start(f32[64,128]{1,0:T(8,128)} %charges.7) | copy-start | bytes 98308
  4.4 5.7 %copy-start.18 = (s32[64]{0:T(128)S(1)}, s32[64]{0:T(128)}, u32[]{:S(2)}) copy-start(s32[64]{0:T(128)} %counts.9) | copy-start | bytes 772
  4.4 25.0 %collective-permute-start = (f32[88,128]{1,0:T(8,128)}, f32[88,128]{1,0:T(8,128)S(1)}, u32[]{:S(2)}, u32[]{:S(2)}) collective-permute-start(f32[88,128]{1,0:T(8,128)} %get-tuple-element.13), channel_id=1, source_target_pairs={{0,1},{1,8},{2,3},{3,10},{4,5},{5,12},{6,7},{7,14},{8,9},{9,64},{1... | collective-permute-start | bytes 135176 | tf_op jit(solution)/shard_map/ppermute | solution.py:672
  4.4 25.0 %collective-permute-start.1 = (f32[88,128]{1,0:T(8,128)}, f32[88,128]{1,0:T(8,128)S(1)}, u32[]{:S(2)}, u32[]{:S(2)}) collective-permute-start(f32[88,128]{1,0:T(8,128)} %get-tuple-element.14), channel_id=1, source_target_pairs={{0,73},{1,0},{2,75},{3,2},{4,77},{5,4},{6,79},{7,6},{8,1},{9,8},{1... | collective-permute-start | bytes 135176 | tf_op jit(solution)/shard_map/ppermute | solution.py:673
  30.1 7.2 %copy-start.4 = (f32[64,128]{1,0:T(8,128)S(1)}, f32[64,128]{1,0:T(8,128)}, u32[]{:S(2)}) copy-start(f32[64,128]{1,0:T(8,128)} %charges.7) | copy-start | bytes 98308
  30.1 7.2 %copy-start.14 = (f32[128,128]{1,0:T(8,128)S(1)}, f32[128,128]{1,0:T(8,128)}, u32[]{:S(2)}) copy-start(f32[128,128]{1,0:T(8,128)} %copy-done.13) | copy-start | bytes 196612
  31.8 5.5 %copy-start.1 = (f32[64,3,128]{2,0,1:T(8,128)S(1)}, f32[64,3,128]{2,0,1:T(8,128)}, u32[]{:S(2)}) copy-start(f32[64,3,128]{2,0,1:T(8,128)} %param.7) | copy-start | bytes 294916
  31.8 26.1 %collective-permute-start.3 = (f32[136,128]{1,0:T(8,128)}, f32[136,128]{1,0:T(8,128)S(1)}, u32[]{:S(2)}, u32[]{:S(2)}) collective-permute-start(f32[136,128]{1,0:T(8,128)} %get-tuple-element.16), channel_id=1, source_target_pairs={{0,146},{1,147},{2,0},{3,1},{4,150},{5,151},{6,4},{7,5},{8,154},{9... | collective-permute-start | bytes 208904 | tf_op jit(solution)/shard_map/ppermute | solution.py:673
  32.0 25.9 %collective-permute-start.2 = (f32[136,128]{1,0:T(8,128)}, f32[136,128]{1,0:T(8,128)S(1)}, u32[]{:S(2)}, u32[]{:S(2)}) collective-permute-start(f32[136,128]{1,0:T(8,128)} %get-tuple-element.15.yup), channel_id=1, source_target_pairs={{0,2},{1,3},{2,16},{3,17},{4,6},{5,7},{6,20},{7,21},{8,10},{9,11},... | collective-permute-start | bytes 208904 | tf_op jit(solution)/shard_map/ppermute | solution.py:672
  37.2 0.7 copy-start.19
  37.9 0.8 copy-start.6
  38.7 0.8 copy-start.8
  39.5 26.9 %copy-start.21 = (s32[6]{0:T(128)}, s32[6]{0:T(128)S(1)}, u32[]{:S(2)}) copy-start(s32[6]{0:T(128)S(1)} %convert_element_type.3.refs_1_.flags) | copy-start | bytes 76
  57.9 8.5 %copy-start.2 = (f32[64,3,128]{2,0,1:T(8,128)S(1)}, f32[64,3,128]{2,0,1:T(8,128)}, u32[]{:S(2)}) copy-start(f32[64,3,128]{2,0,1:T(8,128)} %param.7) | copy-start | bytes 294916
  57.9 8.5 %copy-start.16 = (f32[128,128]{1,0:T(8,128)S(1)}, f32[128,128]{1,0:T(8,128)}, u32[]{:S(2)}) copy-start(f32[128,128]{1,0:T(8,128)} %copy-done.15) | copy-start | bytes 196612
  61.0 5.3 %copy-start.20 = (s32[64]{0:T(128)S(1)}, s32[64]{0:T(128)}, u32[]{:S(2)}) copy-start(s32[64]{0:T(128)} %counts.9) | copy-start | bytes 772
  61.0 21.3 %collective-permute-start.4 = (f32[224,128]{1,0:T(8,128)}, f32[224,128]{1,0:T(8,128)S(1)}, u32[]{:S(2)}, u32[]{:S(2)}) collective-permute-start(f32[224,128]{1,0:T(8,128)} %get-tuple-element.17.zup), channel_id=1, source_target_pairs={{0,4},{1,5},{2,6},{3,7},{4,32},{5,33},{6,34},{7,35},{8,12},{9,13},... | collective-permute-start | bytes 344072 | tf_op jit(solution)/shard_map/ppermute | solution.py:672
  61.3 21.1 %collective-permute-start.5 = (f32[224,128]{1,0:T(8,128)}, f32[224,128]{1,0:T(8,128)S(1)}, u32[]{:S(2)}, u32[]{:S(2)}) collective-permute-start(f32[224,128]{1,0:T(8,128)} %get-tuple-element.18.zdn), channel_id=1, source_target_pairs={{0,36},{1,37},{2,38},{3,39},{4,0},{5,1},{6,2},{7,3},{8,44},{9,45},... | collective-permute-start | bytes 344072 | tf_op jit(solution)/shard_map/ppermute | solution.py:673
  66.4 0.9 copy-start.10
  67.3 0.9 copy-start.12
  81.7 0.6 copy-start.17
  82.3 0.6 copy-start.22
  83.0 0.6 copy-start.23
  (6 other events, 3.7 us)

commit v2 on v1

--- a/solution.py
+++ b/solution.py
@@ -48,31 +48,55 @@
     return jnp.dot(a, b, precision=HIGH, preferred_element_type=F32)
 
 
-def upward_kernel(counts, pos, charges, outer, up_inv, own, xup, xdn, outer_b, source, density):
+def lane_sums(value):
+    return jnp.sum(jnp.transpose(value), axis=0, keepdims=True)
+
+
+TOGETHER_LEAVES = 4
+
+
+def by_fours(leaves, load, work, store):
+    def step(k, carry):
+        at = [k * TOGETHER_LEAVES + u for u in range(TOGETHER_LEAVES)]
+        loaded = [load(i) for i in at]
+        made = [work(*value) for value in loaded]
+        for i, value in zip(at, made):
+            store(i, value)
+        return carry
+
+    lax.fori_loop(0, leaves // TOGETHER_LEAVES, step, 0)
+
+
+def upward_kernel(counts, pos, charges, outer, up_inv, own, xup, xdn, outer_b, source, density, check):
     oc = jnp.transpose(jnp.concatenate([outer[...], jnp.zeros((5, 64), F32)], axis=0))
     for d in range(3):
         outer_b[d] = jnp.broadcast_to(oc[:, d : d + 1], (64, 128))
     lane = lanes((1, 128))
-    lane8 = lanes((64, 128))
-
-    def one(n, check):
-        p = point_rows(pos, n)
-        q = jnp.where(lane < counts[n], charges[pl.ds(n, 1), :], 0.0)
-        source[pl.ds(n, 1), :] = q
+
+    def load(n):
+        return point_rows(pos, n), charges[pl.ds(n, 1), :], counts[n]
+
+    def work(p, charge, count):
+        q = jnp.where(lane < count, charge, 0.0)
         square = SOFTEN
         for d in range(3):
             spread = outer_b[d] - p[d : d + 1]
             square = square + spread * spread
-        col = jnp.sum(lax.rsqrt(square) * q, axis=1, keepdims=True)
-        return jnp.where(lane8 == n, col, check)
-
-    check = lax.fori_loop(0, 64, one, jnp.zeros((64, 128), F32), unroll=4)
-    dens = dot(up_inv[...], check)
-    density[...] = jnp.transpose(jnp.concatenate([dens, jnp.zeros((64, 128), F32)], axis=0))
+        return q, lane_sums(lax.rsqrt(square) * q)
+
+    def store(n, value):
+        source[pl.ds(n, 1), :] = value[0]
+        check[pl.ds(n, 1), :] = value[1]
+
+    by_fours(64, load, work, store)
+    dens = lax.dot_general(
+        check[...], up_inv[...], (((1,), (1,)), ((), ())), precision=HIGH, preferred_element_type=F32
+    )
+    density[...] = jnp.concatenate([dens, dens], axis=1)
     for hz in range(2):
         even = density[pl.ds(2 * hz, 16, stride=4), :]
         odd = density[pl.ds(2 * hz + 1, 16, stride=4), :]
-        own[pl.ds(16 * hz, 16), :] = jnp.where(lane < 64, even, pltpu.roll(odd, 64, 1))
+        own[pl.ds(16 * hz, 16), :] = jnp.where(lane < 64, even, odd)
     for msg, x, xl in ((xup, 3, 2), (xdn, 0, 0)):
         for hz in range(2):
             msg[pl.ds(8 * hz, 8), :] = own[pl.ds(16 * hz + 4 * xl, 8), :]
@@ -94,7 +118,7 @@
             jax.ShapeDtypeStruct((X_ROWS, 128), F32),
         ),
         in_specs=[pl.BlockSpec(memory_space=SMEM)] + [pl.BlockSpec(memory_space=VMEM)] * 4,
-        scratch_shapes=[VMEM((3, 64, 128), F32), VMEM((64, 128), F32), VMEM((128, 128), F32)],
+        scratch_shapes=[VMEM((3, 64, 128), F32), VMEM((64, 128), F32), VMEM((64, 128), F32), VMEM((64, 64), F32)],
         name="upward",
     )(counts, pos, charges, outer, up_inv)
 
@@ -135,6 +159,7 @@
         pack_y_kernel,
         out_shape=(jax.ShapeDtypeStruct((Y_ROWS, 128), F32),) * 2,
         in_specs=[pl.BlockSpec(memory_space=SMEM)] + [pl.BlockSpec(memory_space=VMEM)] * 5 + [pl.BlockSpec(memory_space=pl.ANY)],
+        compiler_params=pltpu.CompilerParams(vmem_limit_bytes=6 * 1024 * 1024),
         name="pack_y",
     )(counts, pos, charges, own, xlo, xhi, near)
 
@@ -175,6 +200,7 @@
         pack_z_kernel,
         out_shape=(jax.ShapeDtypeStruct((Z_ROWS, 128), F32),) * 2,
         in_specs=[pl.BlockSpec(memory_space=SMEM)] + [pl.BlockSpec(memory_space=VMEM)] * 8 + [pl.BlockSpec(memory_space=pl.ANY)],
+        compiler_params=pltpu.CompilerParams(vmem_limit_bytes=6 * 1024 * 1024),
         name="pack_z",
     )(counts, pos, charges, own, xlo, xhi, yup, ylo, yhi, near)
 
@@ -199,77 +225,62 @@
     return jnp.right_shift(n, 4), jnp.bitwise_and(jnp.right_shift(n, 2), 3), jnp.bitwise_and(n, 3)
 
 
-def spread_targets(pos, spread, leaf_of, leaves):
-    row = lax.broadcasted_iota(jnp.int32, (8, 128), 0)
-
-    def one(i, carry):
-        n = leaf_of(i)
-        x, y, z = [c.astype(F32) for c in cell_of(n)]
-        shift = jnp.where(row == 0, x, jnp.where(row == 1, y, z))
-        flat = jnp.concatenate([point_rows(pos, n), jnp.zeros((5, 128), F32)], axis=0) + shift
-        turned = jnp.transpose(flat)
-        for d in range(3):
-            spread[i, d] = jnp.broadcast_to(turned[:, d : d + 1], (128, 128))
+def spread_targets(pos, spread, turned, leaf_of, leaves):
+    number = lax.broadcasted_iota(jnp.int32, (64, 128), 0)
+    for d, part in enumerate(cell_of(number)):
+        flat = pos[d] + part.astype(F32)
+        rest = jnp.transpose(jnp.concatenate([flat, flat], axis=0))[:, :64]
+        for p in range(3):
+            piece = rest.astype(BF16)
+            turned[d, :, pl.ds(64 * p, 64)] = piece
+            rest = rest - piece.astype(F32)
+    place_of = jnp.bitwise_and(lax.broadcasted_iota(jnp.int32, (192, 128), 0), 63)
+
+    def step(k, carry):
+        pick = jnp.concatenate(
+            [jnp.where(place_of == leaf_of(4 * k + u), 1.0, 0.0).astype(BF16) for u in range(4)], axis=1
+        )
+        wide = [jnp.dot(turned[d], pick, preferred_element_type=F32) for d in range(3)]
+        for u in range(4):
+            for d in range(3):
+                spread[4 * k + u, d] = wide[d][:, 128 * u : 128 * (u + 1)]
         return carry
 
-    lax.fori_loop(0, leaves, one, 0, unroll=4)
-
-
-def near_sums(i, count, spread, sums, packed, segments):
+    lax.fori_loop(0, leaves // 4, step, 0)
+
+
+TOGETHER = ((1, 4), (2, 4), (3, 3), (4, 2))
+
+
+def near_sums(i, count, spread, sums, packed, segments, fresh=True):
     lane = lanes((1, 128))
-    tiles, starts, stops, upto = [], [], [], []
-    have = jnp.int32(0)
-    for base, start, stop in segments:
-        first = jnp.right_shift(start, 7)
-        number = jnp.where(stop > start, jnp.right_shift(stop + 127, 7) - first, 0)
-        tiles.append(base + first - have)
-        starts.append(base * 128 + start)
-        stops.append(base * 128 + stop)
-        have = have + number
-        upto.append(have)
-
-    def pick(values, j):
-        value = values[-1]
-        for k in range(len(values) - 2, -1, -1):
-            value = jnp.where(j < upto[k], values[k], value)
-        return value
 
     def run(groups, together):
         rows = pl.ds(0, 8 * groups)
-        blocks = lax.div(have + together - 1, together)
-
-        def ahead(b):
-            squares, charges = [], []
-            for u in range(together):
-                j = b * together + u
-                tile = pick(tiles, j) + jnp.minimum(j, have - 1)
-                at = tile * 128 + lane
-                keep = (at >= pick(starts, j)) & (at < jnp.where(j < have, pick(stops, j), 0))
-                charges.append(jnp.where(keep, packed[tile, pl.ds(3, 1), :], 0.0))
-                square = SOFTEN
-                for d in range(3):
-                    gap = spread[i, d, rows, :] - packed[tile, pl.ds(d, 1), :]
-                    square = square + gap * gap
-                squares.append(square)
-            return squares, charges
-
-        def add(acc, squares, charges):
-            for square, charge in zip(squares, charges):
-                acc = acc + lax.rsqrt(square) * charge
-            return acc
-
-        def step(b, carry):
-            acc, squares, charges = carry
-            later = ahead(b)
-            return (add(acc, squares, charges), *later)
-
-        acc, squares, charges = lax.fori_loop(
-            1, blocks, step, (jnp.zeros((8 * groups, 128), F32), *ahead(0))
-        )
-        sums[i, rows, :] = add(acc, squares, charges)
+        acc = jnp.zeros((8 * groups, 128), F32) if fresh else sums[i, rows, :]
+        for base, start, stop in segments:
+            first = jnp.right_shift(start, 7)
+            last = jnp.right_shift(stop + 127, 7) - 1
+            number = jnp.where(stop > start, last - first + 1, 0)
+
+            def block(b, acc, first=first, last=last, start=start, stop=stop, base=base):
+                for u in range(together):
+                    tile = first + b * together + u
+                    at = lane + tile * 128
+                    where = base + jnp.minimum(tile, last)
+                    charge = jnp.where((at >= start) & (at < stop), packed[where, pl.ds(3, 1), :], 0.0)
+                    square = SOFTEN
+                    for d in range(3):
+                        gap = spread[i, d, rows, :] - packed[where, pl.ds(d, 1), :]
+                        square = square + gap * gap
+                    acc = acc + lax.rsqrt(square) * charge
+                return acc
+
+            acc = lax.fori_loop(0, lax.div(number + together - 1, together), block, acc)
+        sums[i, rows, :] = acc
 
     size = jnp.right_shift(count + 31, 5)
-    for k, together in ((1, 4), (2, 2), (3, 1), (4, 1)):
+    for k, together in TOGETHER:
 
         @pl.when(size == k)
         def _():
@@ -278,20 +289,26 @@
 
 def gather_sums(sums, total, leaf_of, leaves):
     wide = lanes((128, 128))
-
-    def one(i, carry):
-        col = jnp.sum(sums[i], axis=1, keepdims=True)
-        return jnp.where(wide == leaf_of(i), carry + col, carry)
-
-    total[...] = lax.fori_loop(0, leaves, one, total[...], unroll=4)
+    ones = jnp.ones((256, 128), BF16)
+
+    def step(k, carry):
+        value = jnp.concatenate([sums[4 * k + u] for u in range(4)], axis=0)
+        first = value.astype(BF16)
+        second = (value - first.astype(F32)).astype(BF16)
+        column = jnp.dot(jnp.concatenate([first, second], axis=1), ones, preferred_element_type=F32)
+        for u in range(4):
+            carry = jnp.where(wide == leaf_of(4 * k + u), carry + column[128 * u : 128 * (u + 1)], carry)
+        return carry
+
+    total[...] = lax.fori_loop(0, leaves // 4, step, total[...])
 
 
 def near_xy_kernel(windows, *refs):
-    if len(refs) == 9:
-        counts, pos, charges, total, packed, spread, sums, ends, _ = refs
+    if len(refs) == 10:
+        counts, pos, charges, total, packed, spread, turned, sums, ends, _ = refs
         xlo = xhi = None
     else:
-        counts, flags, pos, charges, xlo, xhi, before, total, packed, spread, sums, ends, lo_counts, hi_counts, sem = refs
+        counts, flags, pos, charges, xlo, xhi, before, total, packed, spread, turned, sums, ends, lo_counts, hi_counts, sem = refs
         a = pltpu.make_async_copy(xlo.at[pl.ds(80, 1), :], lo_counts, sem.at[0])
         b = pltpu.make_async_copy(xhi.at[pl.ds(80, 1), :], hi_counts, sem.at[1])
         a.start()
@@ -327,7 +344,7 @@
     def leaf_of(i):
         return jnp.bitwise_and(i, 15) + 16 * (windows[0] + jnp.right_shift(i, 4) * (windows[1] - windows[0]))
 
-    spread_targets(pos, spread, leaf_of, 32)
+    spread_targets(pos, spread, turned, leaf_of, 32)
 
     def leaf_step(i, carry):
         w = jnp.right_shift(i, 4)
@@ -359,6 +376,7 @@
     scratch = [
         VMEM((8 * 16, 8, 128), F32),
         VMEM((32, 3, 128, 128), F32),
+            VMEM((3, 128, 192), BF16),
         VMEM((32, 128, 128), F32),
         SMEM((40,), jnp.int32),
         SMEM((1, 128), F32),
@@ -374,13 +392,13 @@
         out_shape=jax.ShapeDtypeStruct((128, 128), F32),
         in_specs=specs,
         scratch_shapes=scratch,
-        compiler_params=pltpu.CompilerParams(vmem_limit_bytes=24 * 1024 * 1024),
+        compiler_params=pltpu.CompilerParams(vmem_limit_bytes=14 * 1024 * 1024),
         cost_estimate=pl.CostEstimate(flops=150_000_000, bytes_accessed=300_000, transcendentals=10_000_000),
         name="near_x",
     )(*call_args)
 
 
-def near_y_kernel(counts, flags, pos, ylo, yhi, before, total, packed, spread, sums, ends, row_counts, sem):
+def near_y_kernel(counts, flags, pos, ylo, yhi, before, total, packed, spread, turned, sums, ends, row_counts, sem):
     copies = [
         pltpu.make_async_copy(msg.at[pl.ds(128, 8), :], row_counts.at[i], sem.at[i])
         for i, msg in enumerate((ylo, yhi))
@@ -416,7 +434,7 @@
         x = jnp.bitwise_and(jnp.right_shift(i, 2), 3)
         return 16 * x + 12 * side + jnp.bitwise_and(i, 3)
 
-    spread_targets(pos, spread, leaf_of, 32)
+    spread_targets(pos, spread, turned, leaf_of, 32)
 
     def leaf_step(i, carry):
         side = jnp.right_shift(i, 4)
@@ -446,12 +464,13 @@
         scratch_shapes=[
             VMEM((8 * 10, 8, 128), F32),
             VMEM((32, 3, 128, 128), F32),
+            VMEM((3, 128, 192), BF16),
             VMEM((32, 128, 128), F32),
             SMEM((56,), jnp.int32),
             SMEM((2, 8, 128), F32),
             pltpu.SemaphoreType.DMA((2,)),
         ],
-        compiler_params=pltpu.CompilerParams(vmem_limit_bytes=24 * 1024 * 1024),
+        compiler_params=pltpu.CompilerParams(vmem_limit_bytes=14 * 1024 * 1024),
         cost_estimate=pl.CostEstimate(flops=60_000_000, bytes_accessed=300_000, transcendentals=4_000_000),
         name="near_y",
     )(counts, flags, pos, ylo, yhi, before)
@@ -459,7 +478,7 @@
 
 def final_kernel(
     counts, flags, pos, charges, zup, zdn, zlo, zhi, before, inner, outer, down_inv,
-    out, packed, spread, sums, ends, row_counts, total, grid, weights, left, local, sem,
+    out, packed, spread, turned, sums, ends, row_counts, total, grid, weights, left, local, sem,
 ):
     copies = [
         pltpu.make_async_copy(msg.at[pl.ds(208, 16), :], row_counts.at[i], sem.at[i])
@@ -598,41 +617,42 @@
     outer_twice = jnp.concatenate([outer[...], outer[...]], axis=1)
     lane = lanes((1, 128))
 
-    def far_source(n, carry):
+    spread_targets(pos, spread, turned, lambda i: i, 64)
+
+    def far_step(n, carry):
+        cell = cell_of(n)
+        x, y, z = cell
+        weight = local[pl.ds(x * 8 + jnp.right_shift(z, 1) * 4 + y, 1), :]
+        weight = jnp.where(jnp.right_shift(lane, 6) == jnp.bitwise_and(z, 1), weight, 0.0)
+        square = SOFTEN
+        for d in range(3):
+            gap = spread[n, d] - (outer_twice[d : d + 1] + cell[d].astype(F32))
+            square = square + gap * gap
+        sums[n] = lax.rsqrt(square) * weight
+        return carry
+
+    lax.fori_loop(0, 64, far_step, 0, unroll=2)
+
+    def leaf_step(i, carry):
+        side = jnp.bitwise_and(i, 1)
+        n = jnp.right_shift(i, 1) * 4 + 3 * side
         x, y, z = cell_of(n)
-        for d, c in enumerate((x, y, z)):
-            packed[120 + n, pl.ds(d, 1), :] = outer_twice[d : d + 1] + c.astype(F32)
-        weight = local[pl.ds(x * 8 + jnp.right_shift(z, 1) * 4 + y, 1), :]
-        mine = jnp.right_shift(lane, 6) == jnp.bitwise_and(z, 1)
-        packed[120 + n, pl.ds(3, 1), :] = jnp.where(mine, weight, 0.0)
-        return carry
-
-    lax.fori_loop(0, 64, far_source, 0, unroll=8)
-    spread_targets(pos, spread, lambda i: i, 64)
-
-    def leaf_step(n, carry):
-        x, y, z = cell_of(n)
-        side = jnp.right_shift(z, 1)
-        edge = (z == 0) | (z == 3)
-        segments = [(120 + n, jnp.int32(0), jnp.int32(128))]
+        segments = []
         for dy in range(3):
             lst = side * 6 + y + dy
-            start = ends[lst * 7 + x]
-            stop = jnp.where(edge, ends[lst * 7 + x + 3], start)
-            segments.append((lst * 10, start, stop))
-        near_sums(n, counts[n], spread, sums, packed, segments)
+            segments.append((lst * 10, ends[lst * 7 + x], ends[lst * 7 + x + 3]))
+        near_sums(n, counts[n], spread, sums, packed, segments, fresh=False)
         return carry
 
-    lax.fori_loop(0, 64, leaf_step, 0)
+    lax.fori_loop(0, 32, leaf_step, 0)
     gather_sums(sums, total, lambda i: i, 64)
-    both = jnp.transpose(total[...])
     row = lax.broadcasted_iota(jnp.int32, (64, 1), 0)
     full = jnp.zeros((64, 1), jnp.int32)
     for n in range(64):
         full = jnp.where(row == n, counts[n], full)
     live = lanes((64, 128)) < full
     own_term = lax.rsqrt(jnp.full((64, 128), SOFTEN, F32))
-    out[...] = jnp.where(live, both[:64] - own_term * charges[...], 0.0)
+    out[...] = jnp.where(live, jnp.transpose(total[...])[:64] - own_term * charges[...], 0.0)
 
 
 def check_to_local(check, down_inv):
@@ -650,8 +670,9 @@
         out_shape=jax.ShapeDtypeStruct((64, 128), F32),
         in_specs=[pl.BlockSpec(memory_space=SMEM)] * 2 + [pl.BlockSpec(memory_space=VMEM)] * 10,
         scratch_shapes=[
-            VMEM((12 * 10 + 64, 8, 128), F32),
+            VMEM((12 * 10, 8, 128), F32),
             VMEM((64, 3, 128, 128), F32),
+            VMEM((3, 128, 192), BF16),
             VMEM((64, 128, 128), F32),
             SMEM((84,), jnp.int32),
             SMEM((2, 16, 128), F32),
@@ -662,7 +683,7 @@
             VMEM((32, 128), F32),
             pltpu.SemaphoreType.DMA((2,)),
         ],
-        compiler_params=pltpu.CompilerParams(vmem_limit_bytes=56 * 1024 * 1024),
+        compiler_params=pltpu.CompilerParams(vmem_limit_bytes=30 * 1024 * 1024),
         name="final",
     )(counts, flags, pos, charges, zup, zdn, zlo, zhi, before, inner, outer, down_inv)
 

time: 114 us -> 97.5 us (0.86)
  local copies, waits for them, and re-layouts: 9.07 us -> 0.14 us
  Pallas kernels: 86.8 us -> 79.8 us
    unnamed x48 -> x14, local copies, waits for them, and re-layouts: 8.97 us -> 0.03 us
    pallas_call x1, Pallas kernels: 28.7 us -> 24.7 us  [final(): pl.pallas_call(final_kernel, out_shape=jax.ShapeDtypeStruct((64, 128), F3...]
    pallas_call x1, Pallas kernels: 1.86 us -> 0.62 us  [pack_z(): pl.pallas_call(pack_z_kernel, out_shape=(jax.ShapeDtypeStruct((Z_ROWS, 12...]
  transfers between devices with their start and end apart: 6 -> 6, of which waited for: 0 -> 0; matrix products, arithmetic and copies ran while one was open for 0% -> 0% of each run, Pallas kernels for 45% -> 51%
where the time goes in v2:
time: 97.5 us; the launch traced here: 96.7 us
  Pallas kernels  79.8 us (82%)
  starting transfers between devices  16.4 us (17%)
    pallas_call x2, Pallas kernels, near_xy(): pl.pallas_call(body, out_shape=jax.ShapeDtypeStruct((128, 128), F32), in_...  35.7 us
    pallas_call x1, Pallas kernels, final(): pl.pallas_call(final_kernel, out_shape=jax.ShapeDtypeStruct((64, 128), F3...  24.7 us
    pallas_call x1, Pallas kernels, near_y(): pl.pallas_call(near_y_kernel, out_shape=jax.ShapeDtypeStruct((128, 128),...  13.5 us
    ppermute x3, starting transfers between devices, exchange(): lax.ppermute(down, AXES, shifted(dimension, -1))  12 us
    pallas_call x1, Pallas kernels, upward(): pl.pallas_call(upward_kernel, out_shape=(jax.ShapeDtypeStruct((32, 128),...  4.68 us
    ppermute x3, starting transfers between devices, exchange(): lax.ppermute(up, AXES, shifted(dimension, 1))  4.41 us
  transfers between devices with their start and end apart: 6, of which 0 were waited for; matrix products, arithmetic and copies ran while one was open for 0% of the time, Pallas kernels for 51%

profile of v2, /device:TPU:184, one launch (start us, length us, event | category | flops | bytes accessed | tf_op | source)
XLA Modules:
  0.0 96.7 jit_solution(15224931745135440430)
XLA Ops:
  0.0 4.7 %upward.1 = (f32[32,128]{1,0:T(8,128)}, f32[88,128]{1,0:T(8,128)}, f32[88,128]{1,0:T(8,128)}) custom-call(s32[64]{0:T(128)} %counts.9, f32[3,64,128]{2,1,0:T(8,128)} %bitcast.7, f32[64,128]{1,0:T(8,128)} %charges.7, f32[3,64]{1,0:T(4,128)} %outer.3, f32[64,64]{1,0:T(8,128)} %up_inv.1), custom_call_target="tpu_custom_call" | custom-call | tf_op jit(solution)/shard_map/upward/pallas_call | solution.py:113
  4.7 0.0 collective-permute-start
  4.7 5.6 %collective-permute-start.1 = (f32[88,128]{1,0:T(8,128)}, f32[88,128]{1,0:T(8,128)S(1)}, u32[]{:S(2)}, u32[]{:S(2)}) collective-permute-start(f32[88,128]{1,0:T(8,128)} %get-tuple-element.14), channel_id=1, source_target_pairs={{0,73},{1,0},{2,75},{3,2},{4,77},{5,4},{6,79},{7,6},{8,1},{9,8},{1... | collective-permute-start | bytes 135176 | tf_op jit(solution)/shard_map/ppermute | solution.py:694
  10.3 0.0 copy-done.1
  10.4 17.3 %near_x.2.near.refs_6_ = f32[128,128]{1,0:T(8,128)S(1)} custom-call(s32[64]{0:T(128)S(1)} %copy-done.5, f32[3,64,128]{2,1,0:T(8,128)S(1)} %bitcast.8, f32[64,128]{1,0:T(8,128)S(1)} %copy-done.1), custom_call_target="tpu_custom_call" | custom-call | flops 150000000 | bytes 300000 | tf_op jit(solution)/shard_map/near_x/pallas_call | solution.py:390
  27.6 0.0 collective-permute-done.xlo.refs_4_
  27.6 0.0 collective-permute-done.1.xhi.refs_5_
  27.6 0.6 pack_y.1
  28.3 1.1 %collective-permute-start.3 = (f32[136,128]{1,0:T(8,128)S(1)}, f32[136,128]{1,0:T(8,128)S(1)}, u32[]{:S(2)}, u32[]{:S(2)}) collective-permute-start(f32[136,128]{1,0:T(8,128)S(1)} %get-tuple-element.16), channel_id=1, source_target_pairs={{0,146},{1,147},{2,0},{3,1},{4,150},{5,151},{6,4},{7,5},{8,154},{9... | collective-permute-start | bytes 208904 | tf_op jit(solution)/shard_map/ppermute | solution.py:694
  29.4 4.3 %collective-permute-start.2 = (f32[136,128]{1,0:T(8,128)S(1)}, f32[136,128]{1,0:T(8,128)S(1)}, u32[]{:S(2)}, u32[]{:S(2)}) collective-permute-start(f32[136,128]{1,0:T(8,128)S(1)} %get-tuple-element.15.yup), channel_id=1, source_target_pairs={{0,2},{1,3},{2,16},{3,17},{4,6},{5,7},{6,20},{7,21},{8,10},{9,11},... | collective-permute-start | bytes 208904 | tf_op jit(solution)/shard_map/ppermute | solution.py:693
  33.7 0.1 stack.27
  33.8 18.5 %near_x.3.near.before = f32[128,128]{1,0:T(8,128)S(1)} custom-call(s32[64]{0:T(128)S(1)} %copy-done.5, s32[6]{0:T(128)S(1)} %convert_element_type.3.refs_1_.flags, f32[3,64,128]{2,1,0:T(8,128)S(1)} %bitcast.10, f32[64,128]{1,0:T(8,128)S(1)} %copy-done.1, f32[88,128]{1,0:T(8,128)S(1)} %collective-permute-done.xlo.refs_4_, ...), custom_call_target="tpu_custom_call" | custom-call | flops 150000000 | bytes 300000 | tf_op jit(solution)/shard_map/near_x/pallas_call | solution.py:390
  52.3 0.0 collective-permute-done.3.yhi
  52.3 0.0 collective-permute-done.2.ylo
  52.3 0.6 pack_z.1
  52.9 0.1 collective-permute-start.4
  53.0 0.0 copy-start.3
  53.0 0.0 copy-start.4
  53.0 0.0 copy-start.6
  53.0 5.3 %collective-permute-start.5 = (f32[224,128]{1,0:T(8,128)S(1)}, f32[224,128]{1,0:T(8,128)S(1)}, u32[]{:S(2)}, u32[]{:S(2)}) collective-permute-start(f32[224,128]{1,0:T(8,128)S(1)} %get-tuple-element.18.zdn), channel_id=1, source_target_pairs={{0,36},{1,37},{2,38},{3,39},{4,0},{5,1},{6,2},{7,3},{8,44},{9,45},... | collective-permute-start | bytes 344072 | tf_op jit(solution)/shard_map/ppermute | solution.py:694
  58.3 13.5 %near_y.1.before = f32[128,128]{1,0:T(8,128)S(1)} custom-call(s32[64]{0:T(128)S(1)} %copy-done.5, s32[6]{0:T(128)S(1)} %convert_element_type.3.refs_1_.flags, f32[3,64,128]{2,1,0:T(8,128)S(1)} %bitcast.12, f32[136,128]{1,0:T(8,128)S(1)} %collective-permute-done.2.ylo, f32[136,128]{1,0:T(8,128)S(1)} %collective-permute-done.3.yhi, ...), custom_call_target="tpu_custom_call" | custom-call | flops 60000000 | bytes 300000 | tf_op jit(solution)/shard_map/near_y/pallas_call | solution.py:460
  71.8 0.0 collective-permute-done.4.zlo
  71.8 0.0 collective-permute-done.5.zhi
  71.9 24.7 %final.1 = f32[64,128]{1,0:T(8,128)} custom-call(s32[64]{0:T(128)S(1)} %copy-done.5, s32[6]{0:T(128)S(1)} %convert_element_type.3.refs_1_.flags, f32[3,64,128]{2,1,0:T(8,128)S(1)} %bitcast.13, f32[64,128]{1,0:T(8,128)S(1)} %copy-done.1, f32[224,128]{1,0:T(8,128)S(1)} %get-tuple-element.17.zup, f32[224,128]{1,0:T(8,128)S(1)} %get-tuple-element.18.zdn, ...), custom_call_target="tpu_custom_call" | custom-call | tf_op jit(solution)/shard_map/final/pallas_call | solution.py:668
  (11 shorter events, 0.0 us)
Async XLA Ops:
  0.0 10.3 %copy-start = (f32[64,3,128]{2,0,1:T(8,128)S(1)}, f32[64,3,128]{2,0,1:T(8,128)}, u32[]{:S(2)}) copy-start(f32[64,3,128]{2,0,1:T(8,128)} %param.7) | copy-start | bytes 294916
  0.0 10.3 %copy-start.1 = (f32[64,128]{1,0:T(8,128)S(1)}, f32[64,128]{1,0:T(8,128)}, u32[]{:S(2)}) copy-start(f32[64,128]{1,0:T(8,128)} %charges.7) | copy-start | bytes 98308
  4.7 5.7 %copy-start.5 = (s32[64]{0:T(128)S(1)}, s32[64]{0:T(128)}, u32[]{:S(2)}) copy-start(s32[64]{0:T(128)} %counts.9) | copy-start | bytes 772
  4.7 22.9 %collective-permute-start = (f32[88,128]{1,0:T(8,128)}, f32[88,128]{1,0:T(8,128)S(1)}, u32[]{:S(2)}, u32[]{:S(2)}) collective-permute-start(f32[88,128]{1,0:T(8,128)} %get-tuple-element.13), channel_id=1, source_target_pairs={{0,1},{1,8},{2,3},{3,10},{4,5},{5,12},{6,7},{7,14},{8,9},{9,64},{1... | collective-permute-start | bytes 135176 | tf_op jit(solution)/shard_map/ppermute | solution.py:693
  4.7 23.0 %copy-start.2 = (f32[32,128]{1,0:T(8,128)S(1)}, f32[32,128]{1,0:T(8,128)}, u32[]{:S(2)}) copy-start(f32[32,128]{1,0:T(8,128)} %get-tuple-element.12.own) | copy-start | bytes 49156
  4.7 22.9 %collective-permute-start.1 = (f32[88,128]{1,0:T(8,128)}, f32[88,128]{1,0:T(8,128)S(1)}, u32[]{:S(2)}, u32[]{:S(2)}) collective-permute-start(f32[88,128]{1,0:T(8,128)} %get-tuple-element.14), channel_id=1, source_target_pairs={{0,73},{1,0},{2,75},{3,2},{4,77},{5,4},{6,79},{7,6},{8,1},{9,8},{1... | collective-permute-start | bytes 135176 | tf_op jit(solution)/shard_map/ppermute | solution.py:694
  28.3 24.0 %collective-permute-start.3 = (f32[136,128]{1,0:T(8,128)S(1)}, f32[136,128]{1,0:T(8,128)S(1)}, u32[]{:S(2)}, u32[]{:S(2)}) collective-permute-start(f32[136,128]{1,0:T(8,128)S(1)} %get-tuple-element.16), channel_id=1, source_target_pairs={{0,146},{1,147},{2,0},{3,1},{4,150},{5,151},{6,4},{7,5},{8,154},{9... | collective-permute-start | bytes 208904 | tf_op jit(solution)/shard_map/ppermute | solution.py:694
  29.4 22.9 %collective-permute-start.2 = (f32[136,128]{1,0:T(8,128)S(1)}, f32[136,128]{1,0:T(8,128)S(1)}, u32[]{:S(2)}, u32[]{:S(2)}) collective-permute-start(f32[136,128]{1,0:T(8,128)S(1)} %get-tuple-element.15.yup), channel_id=1, source_target_pairs={{0,2},{1,3},{2,16},{3,17},{4,6},{5,7},{6,20},{7,21},{8,10},{9,11},... | collective-permute-start | bytes 208904 | tf_op jit(solution)/shard_map/ppermute | solution.py:693
  52.9 18.9 %collective-permute-start.4 = (f32[224,128]{1,0:T(8,128)S(1)}, f32[224,128]{1,0:T(8,128)S(1)}, u32[]{:S(2)}, u32[]{:S(2)}) collective-permute-start(f32[224,128]{1,0:T(8,128)S(1)} %get-tuple-element.17.zup), channel_id=1, source_target_pairs={{0,4},{1,5},{2,6},{3,7},{4,32},{5,33},{6,34},{7,35},{8,12},{9,13},... | collective-permute-start | bytes 344072 | tf_op jit(solution)/shard_map/ppermute | solution.py:693
  53.0 18.8 %copy-start.3 = (f32[64,64]{1,0:T(8,128)S(1)}, f32[64,64]{1,0:T(8,128)}, u32[]{:S(2)}) copy-start(f32[64,64]{1,0:T(8,128)} %down_inv.1) | copy-start | bytes 49156
  53.0 18.8 %copy-start.4 = (f32[3,64]{1,0:T(4,128)S(1)}, f32[3,64]{1,0:T(4,128)}, u32[]{:S(2)}) copy-start(f32[3,64]{1,0:T(4,128)} %outer.3) | copy-start | bytes 2308
  53.0 18.8 %copy-start.6 = (f32[3,64]{1,0:T(4,128)S(1)}, f32[3,64]{1,0:T(4,128)}, u32[]{:S(2)}) copy-start(f32[3,64]{1,0:T(4,128)} %inner.1) | copy-start | bytes 2308
  53.0 18.8 %collective-permute-start.5 = (f32[224,128]{1,0:T(8,128)S(1)}, f32[224,128]{1,0:T(8,128)S(1)}, u32[]{:S(2)}, u32[]{:S(2)}) collective-permute-start(f32[224,128]{1,0:T(8,128)S(1)} %get-tuple-element.18.zdn), channel_id=1, source_target_pairs={{0,36},{1,37},{2,38},{3,39},{4,0},{5,1},{6,2},{7,3},{8,44},{9,45},... | collective-permute-start | bytes 344072 | tf_op jit(solution)/shard_map/ppermute | solution.py:694

commit v3 on v2

--- a/solution.py
+++ b/solution.py
@@ -48,50 +48,44 @@
     return jnp.dot(a, b, precision=HIGH, preferred_element_type=F32)
 
 
-def lane_sums(value):
-    return jnp.sum(jnp.transpose(value), axis=0, keepdims=True)
-
-
-TOGETHER_LEAVES = 4
-
-
-def by_fours(leaves, load, work, store):
-    def step(k, carry):
-        at = [k * TOGETHER_LEAVES + u for u in range(TOGETHER_LEAVES)]
-        loaded = [load(i) for i in at]
-        made = [work(*value) for value in loaded]
-        for i, value in zip(at, made):
-            store(i, value)
-        return carry
-
-    lax.fori_loop(0, leaves // TOGETHER_LEAVES, step, 0)
-
-
-def upward_kernel(counts, pos, charges, outer, up_inv, own, xup, xdn, outer_b, source, density, check):
+def upward_kernel(counts, pos, charges, outer, up_inv, own, xup, xdn, outer_b, source, density):
     oc = jnp.transpose(jnp.concatenate([outer[...], jnp.zeros((5, 64), F32)], axis=0))
     for d in range(3):
         outer_b[d] = jnp.broadcast_to(oc[:, d : d + 1], (64, 128))
     lane = lanes((1, 128))
 
-    def load(n):
-        return point_rows(pos, n), charges[pl.ds(n, 1), :], counts[n]
-
-    def work(p, charge, count):
-        q = jnp.where(lane < count, charge, 0.0)
-        square = SOFTEN
-        for d in range(3):
-            spread = outer_b[d] - p[d : d + 1]
-            square = square + spread * spread
-        return q, lane_sums(lax.rsqrt(square) * q)
-
-    def store(n, value):
-        source[pl.ds(n, 1), :] = value[0]
-        check[pl.ds(n, 1), :] = value[1]
-
-    by_fours(64, load, work, store)
-    dens = lax.dot_general(
-        check[...], up_inv[...], (((1,), (1,)), ((), ())), precision=HIGH, preferred_element_type=F32
-    )
+    lane8 = lanes((64, 128))
+    ones = jnp.ones((384, 128), BF16)
+
+    def step(k, check):
+        at = [8 * k + u for u in range(8)]
+        loaded = [(point_rows(pos, n), charges[pl.ds(n, 1), :], counts[n]) for n in at]
+        charge_rows, values = [], []
+        for p, charge, count in loaded:
+            q = jnp.where(lane < count, charge, 0.0)
+            square = SOFTEN
+            for d in range(3):
+                spread = outer_b[d] - p[d : d + 1]
+                square = square + spread * spread
+            charge_rows.append(q)
+            values.append(lax.rsqrt(square) * q)
+        rest = jnp.concatenate(values[:4], axis=0)
+        parts = []
+        for _ in range(3):
+            part = rest.astype(BF16)
+            parts.append(part)
+            rest = rest - part.astype(F32)
+        column = jnp.dot(jnp.concatenate(parts, axis=1), ones, preferred_element_type=F32)
+        columns = [column[64 * u : 64 * (u + 1)] for u in range(4)]
+        columns += [jnp.sum(value, axis=1, keepdims=True) for value in values[4:]]
+        for n, column in zip(at, columns):
+            check = jnp.where(lane8 == n, column, check)
+        for n, q in zip(at, charge_rows):
+            source[pl.ds(n, 1), :] = q
+        return check
+
+    check = lax.fori_loop(0, 8, step, jnp.zeros((64, 128), F32))
+    dens = jnp.transpose(dot(up_inv[...], check))[:64]
     density[...] = jnp.concatenate([dens, dens], axis=1)
     for hz in range(2):
         even = density[pl.ds(2 * hz, 16, stride=4), :]
@@ -118,7 +112,7 @@
             jax.ShapeDtypeStruct((X_ROWS, 128), F32),
         ),
         in_specs=[pl.BlockSpec(memory_space=SMEM)] + [pl.BlockSpec(memory_space=VMEM)] * 4,
-        scratch_shapes=[VMEM((3, 64, 128), F32), VMEM((64, 128), F32), VMEM((64, 128), F32), VMEM((64, 64), F32)],
+        scratch_shapes=[VMEM((3, 64, 128), F32), VMEM((64, 128), F32), VMEM((64, 128), F32)],
         name="upward",
     )(counts, pos, charges, outer, up_inv)
 
@@ -232,7 +226,7 @@
         rest = jnp.transpose(jnp.concatenate([flat, flat], axis=0))[:, :64]
         for p in range(3):
             piece = rest.astype(BF16)
-            turned[d, :, pl.ds(64 * p, 64)] = piece
+            turned[pl.ds(128 * d, 128), pl.ds(64 * p, 64)] = piece
             rest = rest - piece.astype(F32)
     place_of = jnp.bitwise_and(lax.broadcasted_iota(jnp.int32, (192, 128), 0), 63)
 
@@ -240,44 +234,78 @@
         pick = jnp.concatenate(
             [jnp.where(place_of == leaf_of(4 * k + u), 1.0, 0.0).astype(BF16) for u in range(4)], axis=1
         )
-        wide = [jnp.dot(turned[d], pick, preferred_element_type=F32) for d in range(3)]
+        wide = jnp.dot(turned[...], pick, preferred_element_type=F32)
         for u in range(4):
             for d in range(3):
-                spread[4 * k + u, d] = wide[d][:, 128 * u : 128 * (u + 1)]
+                spread[4 * k + u, d] = wide[128 * d : 128 * (d + 1), 128 * u : 128 * (u + 1)]
         return carry
 
     lax.fori_loop(0, leaves // 4, step, 0)
 
 
-TOGETHER = ((1, 4), (2, 4), (3, 3), (4, 2))
+TOGETHER = ((1, 4), (2, 2), (3, 2), (4, 1))
 
 
 def near_sums(i, count, spread, sums, packed, segments, fresh=True):
     lane = lanes((1, 128))
+    shifts, starts, stops, upto = [], [], [], []
+    have = jnp.int32(0)
+    for base, start, stop in segments:
+        first = jnp.right_shift(start, 7)
+        number = jnp.where(stop > start, jnp.right_shift(stop + 127, 7) - first, 0)
+        shifts.append(base + first - have)
+        starts.append(base * 128 + start)
+        stops.append(base * 128 + stop)
+        have = have + number
+        upto.append(have)
+
+    def pick(values, tests):
+        value = values[-1]
+        for k in range(len(values) - 2, -1, -1):
+            value = jnp.where(tests[k], values[k], value)
+        return value
 
     def run(groups, together):
         rows = pl.ds(0, 8 * groups)
-        acc = jnp.zeros((8 * groups, 128), F32) if fresh else sums[i, rows, :]
-        for base, start, stop in segments:
-            first = jnp.right_shift(start, 7)
-            last = jnp.right_shift(stop + 127, 7) - 1
-            number = jnp.where(stop > start, last - first + 1, 0)
-
-            def block(b, acc, first=first, last=last, start=start, stop=stop, base=base):
-                for u in range(together):
-                    tile = first + b * together + u
-                    at = lane + tile * 128
-                    where = base + jnp.minimum(tile, last)
-                    charge = jnp.where((at >= start) & (at < stop), packed[where, pl.ds(3, 1), :], 0.0)
-                    square = SOFTEN
-                    for d in range(3):
-                        gap = spread[i, d, rows, :] - packed[where, pl.ds(d, 1), :]
-                        square = square + gap * gap
-                    acc = acc + lax.rsqrt(square) * charge
-                return acc
-
-            acc = lax.fori_loop(0, lax.div(number + together - 1, together), block, acc)
-        sums[i, rows, :] = acc
+        blocks = lax.div(have + together - 1, together)
+
+        def where_is(b):
+            found = []
+            for u in range(together):
+                j = b * together + u
+                inside = jnp.minimum(j, have - 1)
+                tests = [inside < end for end in upto[:-1]]
+                tile = jnp.maximum(pick(shifts, tests) + inside, 0)
+                stop = jnp.where(j < have, pick(stops, tests), 0)
+                found.append((tile, pick(starts, tests) - tile * 128, stop - tile * 128))
+            return found
+
+        def ahead(found):
+            squares, charges = [], []
+            for tile, low, high in found:
+                keep = (lane >= low) & (lane < high)
+                charges.append(jnp.where(keep, packed[tile, pl.ds(3, 1), :], 0.0))
+                square = SOFTEN
+                for d in range(3):
+                    gap = spread[i, d, rows, :] - packed[tile, pl.ds(d, 1), :]
+                    square = square + gap * gap
+                squares.append(square)
+            return squares, charges
+
+        def add(acc, squares, charges):
+            roots = [lax.rsqrt(square) for square in squares]
+            for root, charge in zip(roots, charges):
+                acc = acc + root * charge
+            return acc
+
+        def step(b, carry):
+            acc, squares, charges, found = carry
+            acc = add(acc, squares, charges)
+            return (acc, *ahead(found), where_is(b + 1))
+
+        begin = jnp.zeros((8 * groups, 128), F32) if fresh else sums[i, rows, :]
+        acc, squares, charges, _ = lax.fori_loop(1, blocks, step, (begin, *ahead(where_is(0)), where_is(1)))
+        sums[i, rows, :] = add(acc, squares, charges)
 
     size = jnp.right_shift(count + 31, 5)
     for k, together in TOGETHER:
@@ -292,15 +320,17 @@
     ones = jnp.ones((256, 128), BF16)
 
     def step(k, carry):
-        value = jnp.concatenate([sums[4 * k + u] for u in range(4)], axis=0)
+        value = jnp.concatenate([sums[8 * k + u] for u in range(4)], axis=0)
         first = value.astype(BF16)
         second = (value - first.astype(F32)).astype(BF16)
         column = jnp.dot(jnp.concatenate([first, second], axis=1), ones, preferred_element_type=F32)
-        for u in range(4):
-            carry = jnp.where(wide == leaf_of(4 * k + u), carry + column[128 * u : 128 * (u + 1)], carry)
+        columns = [column[128 * u : 128 * (u + 1)] for u in range(4)]
+        columns += [jnp.sum(sums[8 * k + u], axis=1, keepdims=True) for u in range(4, 8)]
+        for u, column in enumerate(columns):
+            carry = jnp.where(wide == leaf_of(8 * k + u), carry + column, carry)
         return carry
 
-    total[...] = lax.fori_loop(0, leaves // 4, step, total[...])
+    total[...] = lax.fori_loop(0, leaves // 8, step, total[...])
 
 
 def near_xy_kernel(windows, *refs):
@@ -376,7 +406,7 @@
     scratch = [
         VMEM((8 * 16, 8, 128), F32),
         VMEM((32, 3, 128, 128), F32),
-            VMEM((3, 128, 192), BF16),
+            VMEM((384, 192), BF16),
         VMEM((32, 128, 128), F32),
         SMEM((40,), jnp.int32),
         SMEM((1, 128), F32),
@@ -464,7 +494,7 @@
         scratch_shapes=[
             VMEM((8 * 10, 8, 128), F32),
             VMEM((32, 3, 128, 128), F32),
-            VMEM((3, 128, 192), BF16),
+            VMEM((384, 192), BF16),
             VMEM((32, 128, 128), F32),
             SMEM((56,), jnp.int32),
             SMEM((2, 8, 128), F32),
@@ -672,7 +702,7 @@
         scratch_shapes=[
             VMEM((12 * 10, 8, 128), F32),
             VMEM((64, 3, 128, 128), F32),
-            VMEM((3, 128, 192), BF16),
+            VMEM((384, 192), BF16),
             VMEM((64, 128, 128), F32),
             SMEM((84,), jnp.int32),
             SMEM((2, 16, 128), F32),

time: 97.5 us -> 88.6 us (0.909)
  Pallas kernels: 79.8 us -> 71.1 us
    pallas_call x2, Pallas kernels: 35.7 us -> 31.4 us  [near_xy(): pl.pallas_call(body, out_shape=jax.ShapeDtypeStruct((128, 128), F32), in_...]
    pallas_call x1, Pallas kernels: 24.7 us -> 22.2 us  [final(): pl.pallas_call(final_kernel, out_shape=jax.ShapeDtypeStruct((64, 128), F3...]
    pallas_call x1, Pallas kernels: 13.5 us -> 12.3 us  [near_y(): pl.pallas_call(near_y_kernel, out_shape=jax.ShapeDtypeStruct((128, 128),...]
    ppermute x3, starting transfers between devices: 12 us -> 13.1 us  [exchange(): lax.ppermute(down, AXES, shifted(dimension, -1))]
    ppermute x3, starting transfers between devices: 4.41 us -> 3.31 us  [exchange(): lax.ppermute(up, AXES, shifted(dimension, 1))]
  transfers between devices with their start and end apart: 6 -> 6, of which waited for: 0 -> 0; matrix products, arithmetic and copies ran while one was open for 0% -> 0% of each run, Pallas kernels for 51% -> 50%
where the time goes in v3:
time: 88.6 us; the launch traced here: 88 us
  Pallas kernels  71.1 us (80%)
  starting transfers between devices  16.4 us (19%)
    pallas_call x2, Pallas kernels, near_xy(): pl.pallas_call(body, out_shape=jax.ShapeDtypeStruct((128, 128), F32), in_...  31.4 us
    pallas_call x1, Pallas kernels, final(): pl.pallas_call(final_kernel, out_shape=jax.ShapeDtypeStruct((64, 128), F3...  22.2 us
    ppermute x3, starting transfers between devices, exchange(): lax.ppermute(down, AXES, shifted(dimension, -1))  13.1 us
    pallas_call x1, Pallas kernels, near_y(): pl.pallas_call(near_y_kernel, out_shape=jax.ShapeDtypeStruct((128, 128),...  12.3 us
    pallas_call x1, Pallas kernels, upward(): pl.pallas_call(upward_kernel, out_shape=(jax.ShapeDtypeStruct((32, 128),...  3.98 us
    ppermute x3, starting transfers between devices, exchange(): lax.ppermute(up, AXES, shifted(dimension, 1))  3.31 us
  transfers between devices with their start and end apart: 6, of which 0 were waited for; matrix products, arithmetic and copies ran while one was open for 0% of the time, Pallas kernels for 50%

profile of v3, /device:TPU:184, one launch (start us, length us, event | category | flops | bytes accessed | tf_op | source)
XLA Modules:
  0.0 88.0 jit_solution(4107924415284935742)
XLA Ops:
  0.0 4.0 %upward.1 = (f32[32,128]{1,0:T(8,128)}, f32[88,128]{1,0:T(8,128)}, f32[88,128]{1,0:T(8,128)}) custom-call(s32[64]{0:T(128)} %counts.9, f32[3,64,128]{2,1,0:T(8,128)} %bitcast.7, f32[64,128]{1,0:T(8,128)} %charges.7, f32[3,64]{1,0:T(4,128)} %outer.3, f32[64,64]{1,0:T(8,128)} %up_inv.1), custom_call_target="tpu_custom_call" | custom-call | tf_op jit(solution)/shard_map/upward/pallas_call | solution.py:107
  4.0 0.0 collective-permute-start
  4.0 5.6 %collective-permute-start.1 = (f32[88,128]{1,0:T(8,128)}, f32[88,128]{1,0:T(8,128)S(1)}, u32[]{:S(2)}, u32[]{:S(2)}) collective-permute-start(f32[88,128]{1,0:T(8,128)} %get-tuple-element.14), channel_id=1, source_target_pairs={{0,73},{1,0},{2,75},{3,2},{4,77},{5,4},{6,79},{7,6},{8,1},{9,8},{1... | collective-permute-start | bytes 135176 | tf_op jit(solution)/shard_map/ppermute | solution.py:724
  9.7 0.0 copy-done.1
  9.7 15.1 %near_x.2.near.refs_6_ = f32[128,128]{1,0:T(8,128)S(1)} custom-call(s32[64]{0:T(128)S(1)} %copy-done.5, f32[3,64,128]{2,1,0:T(8,128)S(1)} %bitcast.8, f32[64,128]{1,0:T(8,128)S(1)} %copy-done.1), custom_call_target="tpu_custom_call" | custom-call | flops 150000000 | bytes 300000 | tf_op jit(solution)/shard_map/near_x/pallas_call | solution.py:420
  24.8 0.0 collective-permute-done.xlo.refs_4_
  24.8 0.0 collective-permute-done.1.xhi.refs_5_
  24.8 0.6 pack_y.1
  25.5 2.2 %collective-permute-start.3 = (f32[136,128]{1,0:T(8,128)S(1)}, f32[136,128]{1,0:T(8,128)S(1)}, u32[]{:S(2)}, u32[]{:S(2)}) collective-permute-start(f32[136,128]{1,0:T(8,128)S(1)} %get-tuple-element.16), channel_id=1, source_target_pairs={{0,146},{1,147},{2,0},{3,1},{4,150},{5,151},{6,4},{7,5},{8,154},{9... | collective-permute-start | bytes 208904 | tf_op jit(solution)/shard_map/ppermute | solution.py:724
  27.7 3.2 %collective-permute-start.2 = (f32[136,128]{1,0:T(8,128)S(1)}, f32[136,128]{1,0:T(8,128)S(1)}, u32[]{:S(2)}, u32[]{:S(2)}) collective-permute-start(f32[136,128]{1,0:T(8,128)S(1)} %get-tuple-element.15.yup), channel_id=1, source_target_pairs={{0,2},{1,3},{2,16},{3,17},{4,6},{5,7},{6,20},{7,21},{8,10},{9,11},... | collective-permute-start | bytes 208904 | tf_op jit(solution)/shard_map/ppermute | solution.py:723
  30.9 0.1 stack.27
  31.0 16.2 %near_x.3.near.before = f32[128,128]{1,0:T(8,128)S(1)} custom-call(s32[64]{0:T(128)S(1)} %copy-done.5, s32[6]{0:T(128)S(1)} %convert_element_type.3.refs_1_.flags, f32[3,64,128]{2,1,0:T(8,128)S(1)} %bitcast.10, f32[64,128]{1,0:T(8,128)S(1)} %copy-done.1, f32[88,128]{1,0:T(8,128)S(1)} %collective-permute-done.xlo.refs_4_, ...), custom_call_target="tpu_custom_call" | custom-call | flops 150000000 | bytes 300000 | tf_op jit(solution)/shard_map/near_x/pallas_call | solution.py:420
  47.2 0.0 collective-permute-done.3.yhi
  47.3 0.0 collective-permute-done.2.ylo
  47.3 0.6 pack_z.1
  47.9 0.1 collective-permute-start.4
  48.0 0.0 copy-start.3
  48.0 0.0 copy-start.4
  48.0 0.0 copy-start.6
  48.0 5.3 %collective-permute-start.5 = (f32[224,128]{1,0:T(8,128)S(1)}, f32[224,128]{1,0:T(8,128)S(1)}, u32[]{:S(2)}, u32[]{:S(2)}) collective-permute-start(f32[224,128]{1,0:T(8,128)S(1)} %get-tuple-element.18.zdn), channel_id=1, source_target_pairs={{0,36},{1,37},{2,38},{3,39},{4,0},{5,1},{6,2},{7,3},{8,44},{9,45},... | collective-permute-start | bytes 344072 | tf_op jit(solution)/shard_map/ppermute | solution.py:724
  53.3 12.3 %near_y.1.before = f32[128,128]{1,0:T(8,128)S(1)} custom-call(s32[64]{0:T(128)S(1)} %copy-done.5, s32[6]{0:T(128)S(1)} %convert_element_type.3.refs_1_.flags, f32[3,64,128]{2,1,0:T(8,128)S(1)} %bitcast.12, f32[136,128]{1,0:T(8,128)S(1)} %collective-permute-done.2.ylo, f32[136,128]{1,0:T(8,128)S(1)} %collective-permute-done.3.yhi, ...), custom_call_target="tpu_custom_call" | custom-call | flops 60000000 | bytes 300000 | tf_op jit(solution)/shard_map/near_y/pallas_call | solution.py:490
  65.6 0.0 collective-permute-done.4.zlo
  65.6 0.0 collective-permute-done.5.zhi
  65.6 22.2 %final.1 = f32[64,128]{1,0:T(8,128)} custom-call(s32[64]{0:T(128)S(1)} %copy-done.5, s32[6]{0:T(128)S(1)} %convert_element_type.3.refs_1_.flags, f32[3,64,128]{2,1,0:T(8,128)S(1)} %bitcast.13, f32[64,128]{1,0:T(8,128)S(1)} %copy-done.1, f32[224,128]{1,0:T(8,128)S(1)} %get-tuple-element.17.zup, f32[224,128]{1,0:T(8,128)S(1)} %get-tuple-element.18.zdn, ...), custom_call_target="tpu_custom_call" | custom-call | tf_op jit(solution)/shard_map/final/pallas_call | solution.py:698
  (11 shorter events, 0.0 us)
Async XLA Ops:
  0.0 9.7 %copy-start = (f32[64,3,128]{2,0,1:T(8,128)S(1)}, f32[64,3,128]{2,0,1:T(8,128)}, u32[]{:S(2)}) copy-start(f32[64,3,128]{2,0,1:T(8,128)} %param.7) | copy-start | bytes 294916
  0.0 9.7 %copy-start.1 = (f32[64,128]{1,0:T(8,128)S(1)}, f32[64,128]{1,0:T(8,128)}, u32[]{:S(2)}) copy-start(f32[64,128]{1,0:T(8,128)} %charges.7) | copy-start | bytes 98308
  4.0 5.7 %copy-start.5 = (s32[64]{0:T(128)S(1)}, s32[64]{0:T(128)}, u32[]{:S(2)}) copy-start(s32[64]{0:T(128)} %counts.9) | copy-start | bytes 772
  4.0 20.8 %collective-permute-start = (f32[88,128]{1,0:T(8,128)}, f32[88,128]{1,0:T(8,128)S(1)}, u32[]{:S(2)}, u32[]{:S(2)}) collective-permute-start(f32[88,128]{1,0:T(8,128)} %get-tuple-element.13), channel_id=1, source_target_pairs={{0,1},{1,8},{2,3},{3,10},{4,5},{5,12},{6,7},{7,14},{8,9},{9,64},{1... | collective-permute-start | bytes 135176 | tf_op jit(solution)/shard_map/ppermute | solution.py:723
  4.0 20.8 %copy-start.2 = (f32[32,128]{1,0:T(8,128)S(1)}, f32[32,128]{1,0:T(8,128)}, u32[]{:S(2)}) copy-start(f32[32,128]{1,0:T(8,128)} %get-tuple-element.12.own) | copy-start | bytes 49156
  4.0 20.8 %collective-permute-start.1 = (f32[88,128]{1,0:T(8,128)}, f32[88,128]{1,0:T(8,128)S(1)}, u32[]{:S(2)}, u32[]{:S(2)}) collective-permute-start(f32[88,128]{1,0:T(8,128)} %get-tuple-element.14), channel_id=1, source_target_pairs={{0,73},{1,0},{2,75},{3,2},{4,77},{5,4},{6,79},{7,6},{8,1},{9,8},{1... | collective-permute-start | bytes 135176 | tf_op jit(solution)/shard_map/ppermute | solution.py:724
  25.5 21.8 %collective-permute-start.3 = (f32[136,128]{1,0:T(8,128)S(1)}, f32[136,128]{1,0:T(8,128)S(1)}, u32[]{:S(2)}, u32[]{:S(2)}) collective-permute-start(f32[136,128]{1,0:T(8,128)S(1)} %get-tuple-element.16), channel_id=1, source_target_pairs={{0,146},{1,147},{2,0},{3,1},{4,150},{5,151},{6,4},{7,5},{8,154},{9... | collective-permute-start | bytes 208904 | tf_op jit(solution)/shard_map/ppermute | solution.py:724
  27.7 19.6 %collective-permute-start.2 = (f32[136,128]{1,0:T(8,128)S(1)}, f32[136,128]{1,0:T(8,128)S(1)}, u32[]{:S(2)}, u32[]{:S(2)}) collective-permute-start(f32[136,128]{1,0:T(8,128)S(1)} %get-tuple-element.15.yup), channel_id=1, source_target_pairs={{0,2},{1,3},{2,16},{3,17},{4,6},{5,7},{6,20},{7,21},{8,10},{9,11},... | collective-permute-start | bytes 208904 | tf_op jit(solution)/shard_map/ppermute | solution.py:723
  47.9 17.7 %collective-permute-start.4 = (f32[224,128]{1,0:T(8,128)S(1)}, f32[224,128]{1,0:T(8,128)S(1)}, u32[]{:S(2)}, u32[]{:S(2)}) collective-permute-start(f32[224,128]{1,0:T(8,128)S(1)} %get-tuple-element.17.zup), channel_id=1, source_target_pairs={{0,4},{1,5},{2,6},{3,7},{4,32},{5,33},{6,34},{7,35},{8,12},{9,13},... | collective-permute-start | bytes 344072 | tf_op jit(solution)/shard_map/ppermute | solution.py:723
  48.0 17.6 %copy-start.3 = (f32[64,64]{1,0:T(8,128)S(1)}, f32[64,64]{1,0:T(8,128)}, u32[]{:S(2)}) copy-start(f32[64,64]{1,0:T(8,128)} %down_inv.1) | copy-start | bytes 49156
  48.0 17.6 %copy-start.4 = (f32[3,64]{1,0:T(4,128)S(1)}, f32[3,64]{1,0:T(4,128)}, u32[]{:S(2)}) copy-start(f32[3,64]{1,0:T(4,128)} %outer.3) | copy-start | bytes 2308
  48.0 17.6 %copy-start.6 = (f32[3,64]{1,0:T(4,128)S(1)}, f32[3,64]{1,0:T(4,128)}, u32[]{:S(2)}) copy-start(f32[3,64]{1,0:T(4,128)} %inner.1) | copy-start | bytes 2308
  48.0 17.6 %collective-permute-start.5 = (f32[224,128]{1,0:T(8,128)S(1)}, f32[224,128]{1,0:T(8,128)S(1)}, u32[]{:S(2)}, u32[]{:S(2)}) collective-permute-start(f32[224,128]{1,0:T(8,128)S(1)} %get-tuple-element.18.zdn), channel_id=1, source_target_pairs={{0,36},{1,37},{2,38},{3,39},{4,0},{5,1},{6,2},{7,3},{8,44},{9,45},... | collective-permute-start | bytes 344072 | tf_op jit(solution)/shard_map/ppermute | solution.py:724

commit v4 on v3

--- a/solution.py
+++ b/solution.py
@@ -246,7 +246,7 @@
 TOGETHER = ((1, 4), (2, 2), (3, 2), (4, 1))
 
 
-def near_sums(i, count, spread, sums, packed, segments, fresh=True):
+def near_sums(i, count, spread, sums, packed, segments):
     lane = lanes((1, 128))
     shifts, starts, stops, upto = [], [], [], []
     have = jnp.int32(0)
@@ -273,9 +273,9 @@
             found = []
             for u in range(together):
                 j = b * together + u
-                inside = jnp.minimum(j, have - 1)
+                inside = jnp.maximum(jnp.minimum(j, have - 1), 0)
                 tests = [inside < end for end in upto[:-1]]
-                tile = jnp.maximum(pick(shifts, tests) + inside, 0)
+                tile = pick(shifts, tests) + inside
                 stop = jnp.where(j < have, pick(stops, tests), 0)
                 found.append((tile, pick(starts, tests) - tile * 128, stop - tile * 128))
             return found
@@ -303,7 +303,7 @@
             acc = add(acc, squares, charges)
             return (acc, *ahead(found), where_is(b + 1))
 
-        begin = jnp.zeros((8 * groups, 128), F32) if fresh else sums[i, rows, :]
+        begin = jnp.zeros((8 * groups, 128), F32)
         acc, squares, charges, _ = lax.fori_loop(1, blocks, step, (begin, *ahead(where_is(0)), where_is(1)))
         sums[i, rows, :] = add(acc, squares, charges)
 
@@ -508,7 +508,7 @@
 
 def final_kernel(
     counts, flags, pos, charges, zup, zdn, zlo, zhi, before, inner, outer, down_inv,
-    out, packed, spread, turned, sums, ends, row_counts, total, grid, weights, left, local, sem,
+    out, packed, spread, turned, sums, ends, row_counts, total, grid, weights, left, local, far, outer_b, sem,
 ):
     copies = [
         pltpu.make_async_copy(msg.at[pl.ds(208, 16), :], row_counts.at[i], sem.at[i])
@@ -612,7 +612,6 @@
             xs = (0, 1, 2, 3)
         over_x(ox, xs, [x + ox + 2 for x in xs])
     down = check_to_local(jnp.concatenate(check, axis=0), down_inv)
-    local[...] = down
 
     for c in copies:
         c.wait()
@@ -644,45 +643,64 @@
                 ends[lst * 7 + ex + 1] = end
             close_list(packed, lst * 10, end)
 
-    outer_twice = jnp.concatenate([outer[...], outer[...]], axis=1)
-    lane = lanes((1, 128))
-
-    spread_targets(pos, spread, turned, lambda i: i, 64)
-
-    def far_step(n, carry):
-        cell = cell_of(n)
-        x, y, z = cell
-        weight = local[pl.ds(x * 8 + jnp.right_shift(z, 1) * 4 + y, 1), :]
-        weight = jnp.where(jnp.right_shift(lane, 6) == jnp.bitwise_and(z, 1), weight, 0.0)
-        square = SOFTEN
-        for d in range(3):
-            gap = spread[n, d] - (outer_twice[d : d + 1] + cell[d].astype(F32))
-            square = square + gap * gap
-        sums[n] = lax.rsqrt(square) * weight
+    outer_columns = jnp.transpose(jnp.concatenate([outer[...], jnp.zeros((5, 64), F32)], axis=0))
+    for d in range(3):
+        outer_b[d] = jnp.broadcast_to(outer_columns[:, d : d + 1], (64, 128))
+    rest = jnp.transpose(down)
+    parts = []
+    for _ in range(3):
+        part = rest.astype(BF16)
+        parts.append(part)
+        rest = rest - part.astype(F32)
+    local[...] = jnp.concatenate(parts, axis=1)
+    place_of = jnp.bitwise_and(lax.broadcasted_iota(jnp.int32, (96, 128), 0), 31)
+
+    def far_step(k, carry):
+        row = jnp.right_shift(k, 2) * 8 + jnp.bitwise_and(k, 3)
+        pick = jnp.concatenate(
+            [jnp.where(place_of == row + 4 * hz, 1.0, 0.0).astype(BF16) for hz in range(2)], axis=1
+        )
+        weights_of = jnp.dot(local[...], pick, preferred_element_type=F32)
+        points = [point_rows(pos, 4 * k + z) for z in range(4)]
+        made = []
+        for z, p in enumerate(points):
+            square = SOFTEN
+            for d in range(3):
+                gap = p[d : d + 1] - outer_b[d]
+                square = square + gap * gap
+            weight = weights_of[64 * (z % 2) : 64 * (z % 2) + 64, 128 * (z // 2) : 128 * (z // 2) + 128]
+            made.append(jnp.sum(lax.rsqrt(square) * weight, axis=0, keepdims=True))
+        for z, value in enumerate(made):
+            far[pl.ds(4 * k + z, 1), :] = value
         return carry
 
-    lax.fori_loop(0, 64, far_step, 0, unroll=2)
+    lax.fori_loop(0, 16, far_step, 0)
+
+    def leaf_of(i):
+        return jnp.right_shift(i, 1) * 4 + 3 * jnp.bitwise_and(i, 1)
+
+    spread_targets(pos, spread, turned, leaf_of, 32)
 
     def leaf_step(i, carry):
         side = jnp.bitwise_and(i, 1)
-        n = jnp.right_shift(i, 1) * 4 + 3 * side
+        n = leaf_of(i)
         x, y, z = cell_of(n)
         segments = []
         for dy in range(3):
             lst = side * 6 + y + dy
             segments.append((lst * 10, ends[lst * 7 + x], ends[lst * 7 + x + 3]))
-        near_sums(n, counts[n], spread, sums, packed, segments, fresh=False)
+        near_sums(i, counts[n], spread, sums, packed, segments)
         return carry
 
     lax.fori_loop(0, 32, leaf_step, 0)
-    gather_sums(sums, total, lambda i: i, 64)
+    gather_sums(sums, total, leaf_of, 32)
     row = lax.broadcasted_iota(jnp.int32, (64, 1), 0)
     full = jnp.zeros((64, 1), jnp.int32)
     for n in range(64):
         full = jnp.where(row == n, counts[n], full)
     live = lanes((64, 128)) < full
     own_term = lax.rsqrt(jnp.full((64, 128), SOFTEN, F32))
-    out[...] = jnp.where(live, jnp.transpose(total[...])[:64] - own_term * charges[...], 0.0)
+    out[...] = jnp.where(live, jnp.transpose(total[...])[:64] + far[...] - own_term * charges[...], 0.0)
 
 
 def check_to_local(check, down_inv):
@@ -701,19 +719,21 @@
         in_specs=[pl.BlockSpec(memory_space=SMEM)] * 2 + [pl.BlockSpec(memory_space=VMEM)] * 10,
         scratch_shapes=[
             VMEM((12 * 10, 8, 128), F32),
-            VMEM((64, 3, 128, 128), F32),
+            VMEM((32, 3, 128, 128), F32),
             VMEM((384, 192), BF16),
-            VMEM((64, 128, 128), F32),
+            VMEM((32, 128, 128), F32),
             SMEM((84,), jnp.int32),
             SMEM((2, 16, 128), F32),
             VMEM((128, 128), F32),
             VMEM((4, 8, 8, 128), F32),
             VMEM((2688, 256), BF16),
             VMEM((2, 8, 8, 2688), F32),
-            VMEM((32, 128), F32),
+            VMEM((128, 96), BF16),
+            VMEM((64, 128), F32),
+            VMEM((3, 64, 128), F32),
             pltpu.SemaphoreType.DMA((2,)),
         ],
-        compiler_params=pltpu.CompilerParams(vmem_limit_bytes=30 * 1024 * 1024),
+        compiler_params=pltpu.CompilerParams(vmem_limit_bytes=20 * 1024 * 1024),
         name="final",
     )(counts, flags, pos, charges, zup, zdn, zlo, zhi, before, inner, outer, down_inv)
 

time: 88.6 us -> 87.8 us (level); the launches traced: 88 us -> 86 us
  Pallas kernels: 71.1 us -> 69.1 us
    ppermute x3, starting transfers between devices: 3.31 us -> 6 us  [exchange(): lax.ppermute(up, AXES, shifted(dimension, 1))]
    ppermute x3, starting transfers between devices: 13.1 us -> 10.5 us  [exchange(): lax.ppermute(down, AXES, shifted(dimension, -1))]
    pallas_call x1, Pallas kernels: 22.2 us -> 20.1 us  [final(): pl.pallas_call(final_kernel, out_shape=jax.ShapeDtypeStruct((64, 128), F3...]
  transfers between devices with their start and end apart: 6 -> 6, of which waited for: 0 -> 0; matrix products, arithmetic and copies ran while one was open for 0% -> 0% of each run, Pallas kernels for 50% -> 51%
where the time goes in v4:
time: 87.8 us; the launch traced here: 86 us
  Pallas kernels  69.1 us (79%)
  starting transfers between devices  16.5 us (19%)
    pallas_call x2, Pallas kernels, near_xy(): pl.pallas_call(body, out_shape=jax.ShapeDtypeStruct((128, 128), F32), in_...  31.6 us
    pallas_call x1, Pallas kernels, final(): pl.pallas_call(final_kernel, out_shape=jax.ShapeDtypeStruct((64, 128), F3...  20.1 us
    pallas_call x1, Pallas kernels, near_y(): pl.pallas_call(near_y_kernel, out_shape=jax.ShapeDtypeStruct((128, 128),...  12.2 us
    ppermute x3, starting transfers between devices, exchange(): lax.ppermute(down, AXES, shifted(dimension, -1))  10.5 us
    ppermute x3, starting transfers between devices, exchange(): lax.ppermute(up, AXES, shifted(dimension, 1))  6 us
    pallas_call x1, Pallas kernels, upward(): pl.pallas_call(upward_kernel, out_shape=(jax.ShapeDtypeStruct((32, 128),...  3.98 us
  transfers between devices with their start and end apart: 6, of which 0 were waited for; matrix products, arithmetic and copies ran while one was open for 0% of the time, Pallas kernels for 51%

profile of v4, /device:TPU:184, one launch (start us, length us, event | category | flops | bytes accessed | tf_op | source)
XLA Modules:
  0.0 86.0 jit_solution(101301739474284733)
XLA Ops:
  0.0 4.0 %upward.1 = (f32[32,128]{1,0:T(8,128)}, f32[88,128]{1,0:T(8,128)}, f32[88,128]{1,0:T(8,128)}) custom-call(s32[64]{0:T(128)} %counts.9, f32[3,64,128]{2,1,0:T(8,128)} %bitcast.7, f32[64,128]{1,0:T(8,128)} %charges.7, f32[3,64]{1,0:T(4,128)} %outer.3, f32[64,64]{1,0:T(8,128)} %up_inv.1), custom_call_target="tpu_custom_call" | custom-call | tf_op jit(solution)/shard_map/upward/pallas_call | solution.py:107
  4.0 0.0 collective-permute-start
  4.0 5.6 %collective-permute-start.1 = (f32[88,128]{1,0:T(8,128)}, f32[88,128]{1,0:T(8,128)S(1)}, u32[]{:S(2)}, u32[]{:S(2)}) collective-permute-start(f32[88,128]{1,0:T(8,128)} %get-tuple-element.14), channel_id=1, source_target_pairs={{0,73},{1,0},{2,75},{3,2},{4,77},{5,4},{6,79},{7,6},{8,1},{9,8},{1... | collective-permute-start | bytes 135176 | tf_op jit(solution)/shard_map/ppermute | solution.py:744
  9.6 0.0 copy-done
  9.7 0.0 copy-done.1
  9.7 0.0 copy-done.5
  9.7 16.2 %near_x.2.near.refs_6_ = f32[128,128]{1,0:T(8,128)S(1)} custom-call(s32[64]{0:T(128)S(1)} %copy-done.5, f32[3,64,128]{2,1,0:T(8,128)S(1)} %bitcast.8, f32[64,128]{1,0:T(8,128)S(1)} %copy-done.1), custom_call_target="tpu_custom_call" | custom-call | flops 150000000 | bytes 300000 | tf_op jit(solution)/shard_map/near_x/pallas_call | solution.py:420
  25.8 0.0 collective-permute-done.xlo.refs_4_
  25.8 0.0 collective-permute-done.1.xhi.refs_5_
  25.8 0.0 copy-done.2
  25.9 0.6 pack_y.1
  26.5 0.9 collective-permute-start.3
  27.3 4.6 %collective-permute-start.2 = (f32[136,128]{1,0:T(8,128)S(1)}, f32[136,128]{1,0:T(8,128)S(1)}, u32[]{:S(2)}, u32[]{:S(2)}) collective-permute-start(f32[136,128]{1,0:T(8,128)S(1)} %get-tuple-element.15.yup), channel_id=1, source_target_pairs={{0,2},{1,3},{2,16},{3,17},{4,6},{5,7},{6,20},{7,21},{8,10},{9,11},... | collective-permute-start | bytes 208904 | tf_op jit(solution)/shard_map/ppermute | solution.py:743
  31.9 0.1 stack.27
  32.0 15.4 %near_x.3.near.before = f32[128,128]{1,0:T(8,128)S(1)} custom-call(s32[64]{0:T(128)S(1)} %copy-done.5, s32[6]{0:T(128)S(1)} %convert_element_type.3.refs_1_.flags, f32[3,64,128]{2,1,0:T(8,128)S(1)} %bitcast.10, f32[64,128]{1,0:T(8,128)S(1)} %copy-done.1, f32[88,128]{1,0:T(8,128)S(1)} %collective-permute-done.xlo.refs_4_, ...), custom_call_target="tpu_custom_call" | custom-call | flops 150000000 | bytes 300000 | tf_op jit(solution)/shard_map/near_x/pallas_call | solution.py:420
  47.4 0.0 collective-permute-done.3.yhi
  47.4 0.0 collective-permute-done.2.ylo
  47.4 0.6 pack_z.1
  48.1 1.4 %collective-permute-start.4 = (f32[224,128]{1,0:T(8,128)S(1)}, f32[224,128]{1,0:T(8,128)S(1)}, u32[]{:S(2)}, u32[]{:S(2)}) collective-permute-start(f32[224,128]{1,0:T(8,128)S(1)} %get-tuple-element.17.zup), channel_id=1, source_target_pairs={{0,4},{1,5},{2,6},{3,7},{4,32},{5,33},{6,34},{7,35},{8,12},{9,13},... | collective-permute-start | bytes 344072 | tf_op jit(solution)/shard_map/ppermute | solution.py:743
  49.5 4.0 %collective-permute-start.5 = (f32[224,128]{1,0:T(8,128)S(1)}, f32[224,128]{1,0:T(8,128)S(1)}, u32[]{:S(2)}, u32[]{:S(2)}) collective-permute-start(f32[224,128]{1,0:T(8,128)S(1)} %get-tuple-element.18.zdn), channel_id=1, source_target_pairs={{0,36},{1,37},{2,38},{3,39},{4,0},{5,1},{6,2},{7,3},{8,44},{9,45},... | collective-permute-start | bytes 344072 | tf_op jit(solution)/shard_map/ppermute | solution.py:744
  53.5 12.2 %near_y.1.before = f32[128,128]{1,0:T(8,128)S(1)} custom-call(s32[64]{0:T(128)S(1)} %copy-done.5, s32[6]{0:T(128)S(1)} %convert_element_type.3.refs_1_.flags, f32[3,64,128]{2,1,0:T(8,128)S(1)} %bitcast.12, f32[136,128]{1,0:T(8,128)S(1)} %collective-permute-done.2.ylo, f32[136,128]{1,0:T(8,128)S(1)} %collective-permute-done.3.yhi, ...), custom_call_target="tpu_custom_call" | custom-call | flops 60000000 | bytes 300000 | tf_op jit(solution)/shard_map/near_y/pallas_call | solution.py:490
  65.7 0.0 collective-permute-done.4.zlo
  65.7 0.0 collective-permute-done.5.zhi
  65.7 20.1 %final.1 = f32[64,128]{1,0:T(8,128)} custom-call(s32[64]{0:T(128)S(1)} %copy-done.5, s32[6]{0:T(128)S(1)} %convert_element_type.3.refs_1_.flags, f32[3,64,128]{2,1,0:T(8,128)S(1)} %bitcast.13, f32[64,128]{1,0:T(8,128)S(1)} %copy-done.1, f32[224,128]{1,0:T(8,128)S(1)} %get-tuple-element.17.zup, f32[224,128]{1,0:T(8,128)S(1)} %get-tuple-element.18.zdn, ...), custom_call_target="tpu_custom_call" | custom-call | tf_op jit(solution)/shard_map/final/pallas_call | solution.py:716
  (11 shorter events, 0.0 us)
Async XLA Ops:
  0.0 9.7 %copy-start = (f32[64,3,128]{2,0,1:T(8,128)S(1)}, f32[64,3,128]{2,0,1:T(8,128)}, u32[]{:S(2)}) copy-start(f32[64,3,128]{2,0,1:T(8,128)} %param.7) | copy-start | bytes 294916
  0.0 9.7 %copy-start.1 = (f32[64,128]{1,0:T(8,128)S(1)}, f32[64,128]{1,0:T(8,128)}, u32[]{:S(2)}) copy-start(f32[64,128]{1,0:T(8,128)} %charges.7) | copy-start | bytes 98308
  4.0 5.7 %copy-start.5 = (s32[64]{0:T(128)S(1)}, s32[64]{0:T(128)}, u32[]{:S(2)}) copy-start(s32[64]{0:T(128)} %counts.9) | copy-start | bytes 772
  4.0 21.8 %collective-permute-start = (f32[88,128]{1,0:T(8,128)}, f32[88,128]{1,0:T(8,128)S(1)}, u32[]{:S(2)}, u32[]{:S(2)}) collective-permute-start(f32[88,128]{1,0:T(8,128)} %get-tuple-element.13), channel_id=1, source_target_pairs={{0,1},{1,8},{2,3},{3,10},{4,5},{5,12},{6,7},{7,14},{8,9},{9,64},{1... | collective-permute-start | bytes 135176 | tf_op jit(solution)/shard_map/ppermute | solution.py:743
  4.0 21.8 %copy-start.2 = (f32[32,128]{1,0:T(8,128)S(1)}, f32[32,128]{1,0:T(8,128)}, u32[]{:S(2)}) copy-start(f32[32,128]{1,0:T(8,128)} %get-tuple-element.12.own) | copy-start | bytes 49156
  4.0 21.8 %collective-permute-start.1 = (f32[88,128]{1,0:T(8,128)}, f32[88,128]{1,0:T(8,128)S(1)}, u32[]{:S(2)}, u32[]{:S(2)}) collective-permute-start(f32[88,128]{1,0:T(8,128)} %get-tuple-element.14), channel_id=1, source_target_pairs={{0,73},{1,0},{2,75},{3,2},{4,77},{5,4},{6,79},{7,6},{8,1},{9,8},{1... | collective-permute-start | bytes 135176 | tf_op jit(solution)/shard_map/ppermute | solution.py:744
  26.5 20.9 %collective-permute-start.3 = (f32[136,128]{1,0:T(8,128)S(1)}, f32[136,128]{1,0:T(8,128)S(1)}, u32[]{:S(2)}, u32[]{:S(2)}) collective-permute-start(f32[136,128]{1,0:T(8,128)S(1)} %get-tuple-element.16), channel_id=1, source_target_pairs={{0,146},{1,147},{2,0},{3,1},{4,150},{5,151},{6,4},{7,5},{8,154},{9... | collective-permute-start | bytes 208904 | tf_op jit(solution)/shard_map/ppermute | solution.py:744
  27.3 20.1 %collective-permute-start.2 = (f32[136,128]{1,0:T(8,128)S(1)}, f32[136,128]{1,0:T(8,128)S(1)}, u32[]{:S(2)}, u32[]{:S(2)}) collective-permute-start(f32[136,128]{1,0:T(8,128)S(1)} %get-tuple-element.15.yup), channel_id=1, source_target_pairs={{0,2},{1,3},{2,16},{3,17},{4,6},{5,7},{6,20},{7,21},{8,10},{9,11},... | collective-permute-start | bytes 208904 | tf_op jit(solution)/shard_map/ppermute | solution.py:743
  48.1 17.6 %collective-permute-start.4 = (f32[224,128]{1,0:T(8,128)S(1)}, f32[224,128]{1,0:T(8,128)S(1)}, u32[]{:S(2)}, u32[]{:S(2)}) collective-permute-start(f32[224,128]{1,0:T(8,128)S(1)} %get-tuple-element.17.zup), channel_id=1, source_target_pairs={{0,4},{1,5},{2,6},{3,7},{4,32},{5,33},{6,34},{7,35},{8,12},{9,13},... | collective-permute-start | bytes 344072 | tf_op jit(solution)/shard_map/ppermute | solution.py:743
  49.5 16.2 %copy-start.3 = (f32[64,64]{1,0:T(8,128)S(1)}, f32[64,64]{1,0:T(8,128)}, u32[]{:S(2)}) copy-start(f32[64,64]{1,0:T(8,128)} %down_inv.1) | copy-start | bytes 49156
  49.5 16.2 %copy-start.4 = (f32[3,64]{1,0:T(4,128)S(1)}, f32[3,64]{1,0:T(4,128)}, u32[]{:S(2)}) copy-start(f32[3,64]{1,0:T(4,128)} %outer.3) | copy-start | bytes 2308
  49.5 16.2 %copy-start.6 = (f32[3,64]{1,0:T(4,128)S(1)}, f32[3,64]{1,0:T(4,128)}, u32[]{:S(2)}) copy-start(f32[3,64]{1,0:T(4,128)} %inner.1) | copy-start | bytes 2308
  49.5 16.2 %collective-permute-start.5 = (f32[224,128]{1,0:T(8,128)S(1)}, f32[224,128]{1,0:T(8,128)S(1)}, u32[]{:S(2)}, u32[]{:S(2)}) collective-permute-start(f32[224,128]{1,0:T(8,128)S(1)} %get-tuple-element.18.zdn), channel_id=1, source_target_pairs={{0,36},{1,37},{2,38},{3,39},{4,0},{5,1},{6,2},{7,3},{8,44},{9,45},... | collective-permute-start | bytes 344072 | tf_op jit(solution)/shard_map/ppermute | solution.py:744

commit v5 on v4

--- a/solution.py
+++ b/solution.py
@@ -232,15 +232,15 @@
 
     def step(k, carry):
         pick = jnp.concatenate(
-            [jnp.where(place_of == leaf_of(4 * k + u), 1.0, 0.0).astype(BF16) for u in range(4)], axis=1
+            [jnp.where(place_of == leaf_of(8 * k + u), 1.0, 0.0).astype(BF16) for u in range(8)], axis=1
         )
         wide = jnp.dot(turned[...], pick, preferred_element_type=F32)
-        for u in range(4):
+        for u in range(8):
             for d in range(3):
-                spread[4 * k + u, d] = wide[128 * d : 128 * (d + 1), 128 * u : 128 * (u + 1)]
+                spread[8 * k + u, d] = wide[128 * d : 128 * (d + 1), 128 * u : 128 * (u + 1)]
         return carry
 
-    lax.fori_loop(0, leaves // 4, step, 0)
+    lax.fori_loop(0, leaves // 8, step, 0)
 
 
 TOGETHER = ((1, 4), (2, 2), (3, 2), (4, 1))

time: 87.8 us -> 84.9 us (0.967)
  Pallas kernels: 69.1 us -> 67.1 us
    ppermute x3, starting transfers between devices: 6 us -> 3.89 us  [exchange(): lax.ppermute(up, AXES, shifted(dimension, 1))]
    ppermute x3, starting transfers between devices: 10.5 us -> 12.5 us  [exchange(): lax.ppermute(down, AXES, shifted(dimension, -1))]
  transfers between devices with their start and end apart: 6 -> 6, of which waited for: 0 -> 0; matrix products, arithmetic and copies ran while one was open for 0% -> 0% of each run, Pallas kernels for 51% -> 50%
where the time goes in v5:
time: 84.9 us; the launch traced here: 84 us
  Pallas kernels  67.1 us (79%)
  starting transfers between devices  16.4 us (19%)
    pallas_call x2, Pallas kernels, near_xy(): pl.pallas_call(body, out_shape=jax.ShapeDtypeStruct((128, 128), F32), in_...  30.8 us
    pallas_call x1, Pallas kernels, final(): pl.pallas_call(final_kernel, out_shape=jax.ShapeDtypeStruct((64, 128), F3...  19.5 us
    ppermute x3, starting transfers between devices, exchange(): lax.ppermute(down, AXES, shifted(dimension, -1))  12.5 us
    pallas_call x1, Pallas kernels, near_y(): pl.pallas_call(near_y_kernel, out_shape=jax.ShapeDtypeStruct((128, 128),...  11.5 us
    pallas_call x1, Pallas kernels, upward(): pl.pallas_call(upward_kernel, out_shape=(jax.ShapeDtypeStruct((32, 128),...  3.98 us
    ppermute x3, starting transfers between devices, exchange(): lax.ppermute(up, AXES, shifted(dimension, 1))  3.89 us
  transfers between devices with their start and end apart: 6, of which 0 were waited for; matrix products, arithmetic and copies ran while one was open for 0% of the time, Pallas kernels for 50%

profile of v5, /device:TPU:184, one launch (start us, length us, event | category | flops | bytes accessed | tf_op | source)
XLA Modules:
  0.0 84.0 jit_solution(14655829251158017843)
XLA Ops:
  0.0 4.0 %upward.1 = (f32[32,128]{1,0:T(8,128)}, f32[88,128]{1,0:T(8,128)}, f32[88,128]{1,0:T(8,128)}) custom-call(s32[64]{0:T(128)} %counts.9, f32[3,64,128]{2,1,0:T(8,128)} %bitcast.7, f32[64,128]{1,0:T(8,128)} %charges.7, f32[3,64]{1,0:T(4,128)} %outer.3, f32[64,64]{1,0:T(8,128)} %up_inv.1), custom_call_target="tpu_custom_call" | custom-call | tf_op jit(solution)/shard_map/upward/pallas_call | solution.py:107
  4.0 0.0 collective-permute-start
  4.0 5.6 %collective-permute-start.1 = (f32[88,128]{1,0:T(8,128)}, f32[88,128]{1,0:T(8,128)S(1)}, u32[]{:S(2)}, u32[]{:S(2)}) collective-permute-start(f32[88,128]{1,0:T(8,128)} %get-tuple-element.14), channel_id=1, source_target_pairs={{0,73},{1,0},{2,75},{3,2},{4,77},{5,4},{6,79},{7,6},{8,1},{9,8},{1... | collective-permute-start | bytes 135176 | tf_op jit(solution)/shard_map/ppermute | solution.py:744
  9.7 14.6 %near_x.2.near.refs_6_ = f32[128,128]{1,0:T(8,128)S(1)} custom-call(s32[64]{0:T(128)S(1)} %copy-done.5, f32[3,64,128]{2,1,0:T(8,128)S(1)} %bitcast.8, f32[64,128]{1,0:T(8,128)S(1)} %copy-done.1), custom_call_target="tpu_custom_call" | custom-call | flops 150000000 | bytes 300000 | tf_op jit(solution)/shard_map/near_x/pallas_call | solution.py:420
  24.3 0.0 collective-permute-done.xlo.refs_4_
  24.3 0.0 collective-permute-done.1.xhi.refs_5_
  24.3 0.6 pack_y.1
  25.0 1.6 %collective-permute-start.3 = (f32[136,128]{1,0:T(8,128)S(1)}, f32[136,128]{1,0:T(8,128)S(1)}, u32[]{:S(2)}, u32[]{:S(2)}) collective-permute-start(f32[136,128]{1,0:T(8,128)S(1)} %get-tuple-element.16), channel_id=1, source_target_pairs={{0,146},{1,147},{2,0},{3,1},{4,150},{5,151},{6,4},{7,5},{8,154},{9... | collective-permute-start | bytes 208904 | tf_op jit(solution)/shard_map/ppermute | solution.py:744
  26.6 3.8 %collective-permute-start.2 = (f32[136,128]{1,0:T(8,128)S(1)}, f32[136,128]{1,0:T(8,128)S(1)}, u32[]{:S(2)}, u32[]{:S(2)}) collective-permute-start(f32[136,128]{1,0:T(8,128)S(1)} %get-tuple-element.15.yup), channel_id=1, source_target_pairs={{0,2},{1,3},{2,16},{3,17},{4,6},{5,7},{6,20},{7,21},{8,10},{9,11},... | collective-permute-start | bytes 208904 | tf_op jit(solution)/shard_map/ppermute | solution.py:743
  30.4 0.1 stack.27
  30.5 16.2 %near_x.3.near.before = f32[128,128]{1,0:T(8,128)S(1)} custom-call(s32[64]{0:T(128)S(1)} %copy-done.5, s32[6]{0:T(128)S(1)} %convert_element_type.3.refs_1_.flags, f32[3,64,128]{2,1,0:T(8,128)S(1)} %bitcast.10, f32[64,128]{1,0:T(8,128)S(1)} %copy-done.1, f32[88,128]{1,0:T(8,128)S(1)} %collective-permute-done.xlo.refs_4_, ...), custom_call_target="tpu_custom_call" | custom-call | flops 150000000 | bytes 300000 | tf_op jit(solution)/shard_map/near_x/pallas_call | solution.py:420
  46.7 0.0 collective-permute-done.3.yhi
  46.7 0.0 collective-permute-done.2.ylo
  46.7 0.6 pack_z.1
  47.3 0.1 collective-permute-start.4
  47.4 0.0 copy-start.3
  47.4 0.0 copy-start.4
  47.4 0.0 copy-start.6
  47.4 5.3 %collective-permute-start.5 = (f32[224,128]{1,0:T(8,128)S(1)}, f32[224,128]{1,0:T(8,128)S(1)}, u32[]{:S(2)}, u32[]{:S(2)}) collective-permute-start(f32[224,128]{1,0:T(8,128)S(1)} %get-tuple-element.18.zdn), channel_id=1, source_target_pairs={{0,36},{1,37},{2,38},{3,39},{4,0},{5,1},{6,2},{7,3},{8,44},{9,45},... | collective-permute-start | bytes 344072 | tf_op jit(solution)/shard_map/ppermute | solution.py:744
  52.7 11.5 %near_y.1.before = f32[128,128]{1,0:T(8,128)S(1)} custom-call(s32[64]{0:T(128)S(1)} %copy-done.5, s32[6]{0:T(128)S(1)} %convert_element_type.3.refs_1_.flags, f32[3,64,128]{2,1,0:T(8,128)S(1)} %bitcast.12, f32[136,128]{1,0:T(8,128)S(1)} %collective-permute-done.2.ylo, f32[136,128]{1,0:T(8,128)S(1)} %collective-permute-done.3.yhi, ...), custom_call_target="tpu_custom_call" | custom-call | flops 60000000 | bytes 300000 | tf_op jit(solution)/shard_map/near_y/pallas_call | solution.py:490
  64.3 0.0 collective-permute-done.4.zlo
  64.3 0.0 collective-permute-done.5.zhi
  64.3 0.0 copy-done.3
  64.3 19.5 %final.1 = f32[64,128]{1,0:T(8,128)} custom-call(s32[64]{0:T(128)S(1)} %copy-done.5, s32[6]{0:T(128)S(1)} %convert_element_type.3.refs_1_.flags, f32[3,64,128]{2,1,0:T(8,128)S(1)} %bitcast.13, f32[64,128]{1,0:T(8,128)S(1)} %copy-done.1, f32[224,128]{1,0:T(8,128)S(1)} %get-tuple-element.17.zup, f32[224,128]{1,0:T(8,128)S(1)} %get-tuple-element.18.zdn, ...), custom_call_target="tpu_custom_call" | custom-call | tf_op jit(solution)/shard_map/final/pallas_call | solution.py:716
  (11 shorter events, 0.0 us)
Async XLA Ops:
  0.0 9.7 %copy-start = (f32[64,3,128]{2,0,1:T(8,128)S(1)}, f32[64,3,128]{2,0,1:T(8,128)}, u32[]{:S(2)}) copy-start(f32[64,3,128]{2,0,1:T(8,128)} %param.7) | copy-start | bytes 294916
  0.0 9.7 %copy-start.1 = (f32[64,128]{1,0:T(8,128)S(1)}, f32[64,128]{1,0:T(8,128)}, u32[]{:S(2)}) copy-start(f32[64,128]{1,0:T(8,128)} %charges.7) | copy-start | bytes 98308
  4.0 5.7 %copy-start.5 = (s32[64]{0:T(128)S(1)}, s32[64]{0:T(128)}, u32[]{:S(2)}) copy-start(s32[64]{0:T(128)} %counts.9) | copy-start | bytes 772
  4.0 20.3 %collective-permute-start = (f32[88,128]{1,0:T(8,128)}, f32[88,128]{1,0:T(8,128)S(1)}, u32[]{:S(2)}, u32[]{:S(2)}) collective-permute-start(f32[88,128]{1,0:T(8,128)} %get-tuple-element.13), channel_id=1, source_target_pairs={{0,1},{1,8},{2,3},{3,10},{4,5},{5,12},{6,7},{7,14},{8,9},{9,64},{1... | collective-permute-start | bytes 135176 | tf_op jit(solution)/shard_map/ppermute | solution.py:743
  4.0 20.3 %copy-start.2 = (f32[32,128]{1,0:T(8,128)S(1)}, f32[32,128]{1,0:T(8,128)}, u32[]{:S(2)}) copy-start(f32[32,128]{1,0:T(8,128)} %get-tuple-element.12.own) | copy-start | bytes 49156
  4.0 20.3 %collective-permute-start.1 = (f32[88,128]{1,0:T(8,128)}, f32[88,128]{1,0:T(8,128)S(1)}, u32[]{:S(2)}, u32[]{:S(2)}) collective-permute-start(f32[88,128]{1,0:T(8,128)} %get-tuple-element.14), channel_id=1, source_target_pairs={{0,73},{1,0},{2,75},{3,2},{4,77},{5,4},{6,79},{7,6},{8,1},{9,8},{1... | collective-permute-start | bytes 135176 | tf_op jit(solution)/shard_map/ppermute | solution.py:744
  25.0 21.7 %collective-permute-start.3 = (f32[136,128]{1,0:T(8,128)S(1)}, f32[136,128]{1,0:T(8,128)S(1)}, u32[]{:S(2)}, u32[]{:S(2)}) collective-permute-start(f32[136,128]{1,0:T(8,128)S(1)} %get-tuple-element.16), channel_id=1, source_target_pairs={{0,146},{1,147},{2,0},{3,1},{4,150},{5,151},{6,4},{7,5},{8,154},{9... | collective-permute-start | bytes 208904 | tf_op jit(solution)/shard_map/ppermute | solution.py:744
  26.6 20.1 %collective-permute-start.2 = (f32[136,128]{1,0:T(8,128)S(1)}, f32[136,128]{1,0:T(8,128)S(1)}, u32[]{:S(2)}, u32[]{:S(2)}) collective-permute-start(f32[136,128]{1,0:T(8,128)S(1)} %get-tuple-element.15.yup), channel_id=1, source_target_pairs={{0,2},{1,3},{2,16},{3,17},{4,6},{5,7},{6,20},{7,21},{8,10},{9,11},... | collective-permute-start | bytes 208904 | tf_op jit(solution)/shard_map/ppermute | solution.py:743
  47.3 17.0 %collective-permute-start.4 = (f32[224,128]{1,0:T(8,128)S(1)}, f32[224,128]{1,0:T(8,128)S(1)}, u32[]{:S(2)}, u32[]{:S(2)}) collective-permute-start(f32[224,128]{1,0:T(8,128)S(1)} %get-tuple-element.17.zup), channel_id=1, source_target_pairs={{0,4},{1,5},{2,6},{3,7},{4,32},{5,33},{6,34},{7,35},{8,12},{9,13},... | collective-permute-start | bytes 344072 | tf_op jit(solution)/shard_map/ppermute | solution.py:743
  47.4 16.9 %copy-start.3 = (f32[64,64]{1,0:T(8,128)S(1)}, f32[64,64]{1,0:T(8,128)}, u32[]{:S(2)}) copy-start(f32[64,64]{1,0:T(8,128)} %down_inv.1) | copy-start | bytes 49156
  47.4 16.9 %copy-start.4 = (f32[3,64]{1,0:T(4,128)S(1)}, f32[3,64]{1,0:T(4,128)}, u32[]{:S(2)}) copy-start(f32[3,64]{1,0:T(4,128)} %outer.3) | copy-start | bytes 2308
  47.4 16.9 %copy-start.6 = (f32[3,64]{1,0:T(4,128)S(1)}, f32[3,64]{1,0:T(4,128)}, u32[]{:S(2)}) copy-start(f32[3,64]{1,0:T(4,128)} %inner.1) | copy-start | bytes 2308
  47.4 16.9 %collective-permute-start.5 = (f32[224,128]{1,0:T(8,128)S(1)}, f32[224,128]{1,0:T(8,128)S(1)}, u32[]{:S(2)}, u32[]{:S(2)}) collective-permute-start(f32[224,128]{1,0:T(8,128)S(1)} %get-tuple-element.18.zdn), channel_id=1, source_target_pairs={{0,36},{1,37},{2,38},{3,39},{4,0},{5,1},{6,2},{7,3},{8,44},{9,45},... | collective-permute-start | bytes 344072 | tf_op jit(solution)/shard_map/ppermute | solution.py:744
